TPU v7x, 128 devices: a whole 4x4x4 slice. The times are simulated.
128 devices in a mesh: inner: 32 (over z, x, core), outer: 4 (over y).
Axes of the slice: x: 4, y: 4, z: 4, core: 2. Of those that a mesh axis runs over, the one named last changes fastest.
Arguments:
- points: bfloat16 [4, 524288, 64], P('outer', 'inner'), may hold values from -1.5 to 1.5
- charges: bfloat16 [4, 524288, 16], P('outer', 'inner'), may hold values from -6 to 6
- bases: bfloat16 [4, 524288, 128], P('outer', 'inner'), may hold values from -0.25 to 0.25
- transfers: bfloat16 [4, 1024, 128, 128], P('outer', 'inner'), may hold values from -0.5 to 0.5
- parents: bfloat16 [4, 32, 128, 128], P('outer', 'inner'), may hold values from -0.5 to 0.5
- couplings: bfloat16 [4, 192, 128, 128], P('outer', 'inner'), may hold values from -0.0390625 to 0.0390625
- group_couplings: bfloat16 [4, 4, 128, 128], P('outer'), may hold values from -0.009765625 to 0.009765625
- near_pairs: int32 [4, 3072, 2], P('outer', 'inner'), may hold values from 0 to 39, as said below
- pair_count: int32 [4, 32], P('outer', 'inner'), may hold values from 1 to 96, as said below
- far_list: int32 [4, 192], P('outer', 'inner'), may hold values from 0 to 31, as said below
Outputs:
- potentials: float32 [4, 524288, 16], P('outer', 'inner')
Inputs may be any that keep to these rules, and one draw needn't show every extreme that they name: `near_pairs`: slot (a, b): a is a holder's leaf; b < 4 names the left inner neighbour's leaf 32 - 4 + b, 4 <= b < 36 the holder's own leaf b - 4 (never a), larger b the right neighbour's leaf b - 36. The first holder of a group names no left neighbour, the last no right one. Slots past the count hold such pairs too and are ignored. `pair_count`: in every group some holder has all 96 slots live. `far_list`: entries are inner indices of nodes in the same group, distinct within a node's list and never the node itself.
All inputs are finite; a program needn't handle non-finite values.
Results may differ from a plain program's by a relative error of at most 0.006.
Values may be sent and summed in bfloat16 or wider, within the bound.
A program may use at most 128 MiB of HBM per device.

v0:
```python
import jax
import jax.numpy as jnp
from jax import lax
from jax.sharding import PartitionSpec as P

REACH = 4
PAIR_BLOCK = 8


INV_TWO_BAND = 0.5
RIDGE = 0.25


def with_halo(block, sides, width):
    for axis, dim in sides:
        count = lax.axis_size(axis)
        forward = [(i, i + 1) for i in range(count - 1)]
        backward = [(target, source) for source, target in forward]
        low = lax.ppermute(
            lax.slice_in_dim(block, block.shape[dim] - width, None, axis=dim), axis, forward
        )
        high = lax.ppermute(lax.slice_in_dim(block, 0, width, axis=dim), axis, backward)
        block = jnp.concatenate([low, block, high], axis=dim)
    return block


def kernel_tiles(left_samples, right_samples):
    left_square = jnp.sum(jnp.square(left_samples.astype(jnp.float32)), -1)
    right_square = jnp.sum(jnp.square(right_samples.astype(jnp.float32)), -1)
    cross_kernel = jnp.einsum(
        "nom,nwm->now", left_samples, right_samples, preferred_element_type=jnp.float32
    )
    distance = left_square[:, :, None] + right_square[:, None, :] - 2.0 * cross_kernel
    return jnp.exp(-INV_TWO_BAND * distance).astype(jnp.bfloat16)


def diag_block(operands):
    block_points, block_charges = operands
    kernel = kernel_tiles(block_points, block_points)
    return jnp.einsum("bpq,bqn->bpn", kernel, block_charges, preferred_element_type=jnp.float32)


def on_device(
    points,
    charges,
    bases,
    transfers,
    parents,
    couplings,
    group_couplings,
    near_pairs,
    pair_count,
    far_list,
):
    leaves = transfers.shape[1]
    leaf_size = points.shape[1] // leaves
    feature_dim = points.shape[2]
    rhs_count = charges.shape[2]
    skeleton_rank = bases.shape[2]
    widened_count = leaves + 2 * REACH
    joined = jnp.concatenate([points[0], charges[0]], 1)[None]
    widened = with_halo(joined, (("inner", 1),), REACH * leaf_size)[0]
    widened = widened.reshape(widened_count, leaf_size, feature_dim + rhs_count)
    own_pairs = near_pairs[0]
    live_count = pair_count[0, 0]
    start = jnp.zeros((widened_count, leaf_size, rhs_count), jnp.float32)
    widened_points = widened[:, :, :feature_dim]
    widened_charges = widened[:, :, feature_dim:]
    pair_blocks = own_pairs.reshape(-1, PAIR_BLOCK, 2)

    def one_block(block_index, totals):
        chosen = lax.dynamic_index_in_dim(pair_blocks, block_index, 0, keepdims=False)
        first_slot = chosen[:, 0] + REACH
        second_slot = chosen[:, 1]
        slot_ids = block_index * PAIR_BLOCK + jnp.arange(PAIR_BLOCK, dtype=jnp.int32)
        live_mask = (slot_ids < live_count).astype(jnp.float32)[:, None, None]
        kernel = kernel_tiles(widened_points[first_slot], widened_points[second_slot])
        to_first = jnp.einsum(
            "bpq,bqn->bpn", kernel, widened_charges[second_slot], preferred_element_type=jnp.float32
        )
        to_second = jnp.einsum(
            "bpq,bpn->bqn", kernel, widened_charges[first_slot], preferred_element_type=jnp.float32
        )
        totals = totals.at[first_slot].add(to_first * live_mask)
        return totals.at[second_slot].add(to_second * live_mask)

    totals = lax.fori_loop(0, pair_blocks.shape[0], one_block, start)
    own_points = points[0].reshape(-1, PAIR_BLOCK, leaf_size, feature_dim)
    own_charges = charges[0].reshape(-1, PAIR_BLOCK, leaf_size, rhs_count)
    diagonal = lax.map(diag_block, (own_points, own_charges)).reshape(leaves * leaf_size, rhs_count)
    rim_rows = REACH * leaf_size
    outgoing = jnp.concatenate([totals[:REACH], totals[REACH + leaves :]], 0).reshape(
        2 * rim_rows, rhs_count
    )
    incoming = with_halo(outgoing, (("inner", 0),), rim_rows)
    near_field = totals[REACH : REACH + leaves].reshape(leaves * leaf_size, rhs_count) + diagonal
    near_field = near_field.at[:rim_rows].add(incoming[:rim_rows])
    near_field = near_field.at[near_field.shape[0] - rim_rows :].add(
        incoming[incoming.shape[0] - rim_rows :]
    )
    leaf_bases = bases[0].reshape(leaves, leaf_size, skeleton_rank)
    charge_leaves = charges[0].reshape(leaves, leaf_size, rhs_count)
    leaf_skeleton = jnp.einsum(
        "lpr,lpn->lrn", leaf_bases, charge_leaves, preferred_element_type=jnp.float32
    ).astype(jnp.bfloat16)
    node_skeleton = jnp.einsum(
        "lrs,lrn->sn", transfers[0], leaf_skeleton, preferred_element_type=jnp.float32
    ).astype(jnp.bfloat16)
    parent_map = parents[0, 0]
    group_term = jnp.einsum(
        "rs,rn->sn", parent_map, node_skeleton, preferred_element_type=jnp.float32
    )
    all_nodes = lax.all_gather(node_skeleton[None], "inner", axis=0, tiled=True)
    group_total = lax.psum(group_term, "inner")
    groups = lax.all_gather(group_total.astype(jnp.bfloat16)[None], "outer", axis=0, tiled=True)
    own_group = lax.axis_index("outer")
    others = (jnp.arange(lax.axis_size("outer"), dtype=jnp.int32) != own_group).astype(jnp.bfloat16)
    masked_couplings = group_couplings[0] * others[:, None, None]
    group_field = jnp.einsum(
        "hrs,hsn->rn", masked_couplings, groups, preferred_element_type=jnp.float32
    ).astype(jnp.bfloat16)
    chosen_nodes = all_nodes[far_list[0]]
    node_field = jnp.einsum(
        "jrs,jsn->rn", couplings[0], chosen_nodes, preferred_element_type=jnp.float32
    )
    node_field = node_field + jnp.einsum(
        "rs,sn->rn", parent_map, group_field, preferred_element_type=jnp.float32
    )
    node_field = node_field.astype(jnp.bfloat16)
    leaf_field = jnp.einsum(
        "lrs,sn->lrn", transfers[0], node_field, preferred_element_type=jnp.float32
    ).astype(jnp.bfloat16)
    far_field = jnp.einsum(
        "lpr,lrn->lpn", leaf_bases, leaf_field, preferred_element_type=jnp.float32
    ).reshape(leaves * leaf_size, rhs_count)
    result = RIDGE * charges[0].astype(jnp.float32) + near_field + far_field
    return result[None]


def solution(mesh):
    placed = (
        P("outer", "inner", None),
        P("outer", "inner", None),
        P("outer", "inner", None),
        P("outer", "inner", None, None),
        P("outer", "inner", None, None),
        P("outer", "inner", None, None),
        P("outer", None, None, None),
        P("outer", "inner", None),
        P("outer", "inner"),
        P("outer", "inner"),
    )
    return jax.shard_map(
        on_device, mesh=mesh, in_specs=placed, out_specs=P("outer", "inner", None), check_vma=False
    )
```

profile of v0, /device:TPU:16, one launch (start us, length us, event | category | flops | bytes accessed | tf_op | source)
XLA Modules:
  0.0 502.8 jit_solution(2174498369405540130)
XLA Ops:
  12.0 26.1 %while.28 = (s32[]{:T(128)}, f32[4,8,512,16]{2,1,0,3:T(8,128)S(1)}, bf16[4,8,512,64]{3,2,1,0:T(8,128)(2,1)}, bf16[4,8,512,16]{2,1,0,3:T(8,128)(2,1)S(1)}, s32[]{:T(128)}) while((s32[]{:T(128)}, f32[4,8,512,16]{2,1,0,3:T(8,128)S(1)}, bf16[4,8,512,64]{3,2,1,0:T(8,128)(2,1)}, bf16[4,8,512,16]{2,1,0,3:T(8,128)(2,1)S(1)}, s32[]{:T(128)}) %tuple.75), condition=%wide.region_8.9_spmd, body=%wide.region_6.8_spmd.sunk | while | flops 346812416 | bytes 2802249 | solution.py:90
  13.9 4.4 fusion.71
  20.4 4.5 fusion.71
  27.0 4.5 fusion.71
  33.6 4.4 fusion.71
  43.0 29.9 %all-gather = bf16[4096,16]{0,1:T(8,128)(2,1)S(1)} all-gather(bf16[128,16]{0,1:T(8,128)(2,1)S(1)} %bitcast.179), channel_id=2, replica_groups=mesh['inner'=32,'outer'=4] {'inner'}, dimensions={0}, use_global_device_ids=true | all-gather | bytes 135168 | tf_op jit(solution)/shard_map/all_gather | solution.py:113
  73.1 66.3 %psum.7 = bf16[128,16]{0,1:T(8,128)(2,1)S(1)} all-reduce(f32[128,16]{0,1:T(8,128)S(1)} %convolution_bitcast_fusion.2), channel_id=1, replica_groups=mesh['inner'=32,'outer'=4] {'inner'}, use_global_device_ids=true, to_apply=%region_9.10 | all-reduce | flops 2048 | bytes 12288 | tf_op jit(solution)/shard_map/psum | solution.py:114
  139.4 10.3 %all-gather.1 = bf16[512,16]{0,1:T(8,128)(2,1)S(1)} all-gather(bf16[128,16]{0,1:T(8,128)(2,1)S(1)} %psum.7), channel_id=3, replica_groups=mesh['inner'=32,'outer'=4] {'outer'}, dimensions={0}, use_global_device_ids=true | all-gather | bytes 20480 | tf_op jit(solution)/shard_map/all_gather | solution.py:115
  160.6 6.5 %copy.22 = bf16[40,512,64]{2,1,0:T(8,128)(2,1)} copy(bf16[40,512,64]{1,0,2:T(8,128)(2,1)} %slice.110) | data formatting | bytes 5242880 | tf_op jit(solution)/shard_map/while | solution.py:87
  167.5 329.1 %while.27 = (s32[]{:T(128)}, f32[40,512,16]{1,2,0:T(8,128)S(1)}, s32[12,8,2]{1,0,2:T(8,128)S(1)}, bf16[40,512,64]{2,1,0:T(8,128)(2,1)}, bf16[40,512,16]{1,2,0:T(...) while((s32[]{:T(128)}, f32[40,512,16]{1,2,0:T(8,128)S(1)}, s32[12,8,2]{1,0,2:T(8,128)S(1)}, ...), condition=%wide.region_5.6_spmd, body=%wide.region_0.5_spmd.sunk | while | flops 414967904 | bytes 19735244 | solution.py:87
  179.5 5.6 %exponential_convert_fusion.7 = bf16[8,512,512]{2,1,0:T(8,128)(2,1)} fusion(f32[8,512]{1,0:T(8,128)S(1)} %multiply_reduce_fusion.6, f32[8,512]{1,0:T(8,128)S(1)} %multiply_reduce_fusion.7, bf16[8,512,64]{2,1,0:T(8,128)(2,1)} %gather_fusion.1, bf16[8,512,64]{2,1,0:T(8,128)(2,1)} %gather_fusion), kind=kOutput, calls=%fused_computation.20.clone.1 | convolution fusion | flops 278921216 | bytes 5275648 | tf_op jit(solution)/shard_map/while/body/eval_jaxpr/nom,nwm->now/dot_general | solution.py:30
  195.0 4.1 gather_fusion
  207.0 5.6 %exponential_convert_fusion.7 = bf16[8,512,512]{2,1,0:T(8,128)(2,1)} fusion(f32[8,512]{1,0:T(8,128)S(1)} %multiply_reduce_fusion.6, f32[8,512]{1,0:T(8,128)S(1)} %multiply_reduce_fusion.7, bf16[8,512,64]{2,1,0:T(8,128)(2,1)} %gather_fusion.1, bf16[8,512,64]{2,1,0:T(8,128)(2,1)} %gather_fusion), kind=kOutput, calls=%fused_computation.20.clone.1 | convolution fusion | flops 278921216 | bytes 5275648 | tf_op jit(solution)/shard_map/while/body/eval_jaxpr/nom,nwm->now/dot_general | solution.py:30
  234.4 5.6 %exponential_convert_fusion.7 = bf16[8,512,512]{2,1,0:T(8,128)(2,1)} fusion(f32[8,512]{1,0:T(8,128)S(1)} %multiply_reduce_fusion.6, f32[8,512]{1,0:T(8,128)S(1)} %multiply_reduce_fusion.7, bf16[8,512,64]{2,1,0:T(8,128)(2,1)} %gather_fusion.1, bf16[8,512,64]{2,1,0:T(8,128)(2,1)} %gather_fusion), kind=kOutput, calls=%fused_computation.20.clone.1 | convolution fusion | flops 278921216 | bytes 5275648 | tf_op jit(solution)/shard_map/while/body/eval_jaxpr/nom,nwm->now/dot_general | solution.py:30
  249.8 4.1 gather_fusion
  261.8 5.6 %exponential_convert_fusion.7 = bf16[8,512,512]{2,1,0:T(8,128)(2,1)} fusion(f32[8,512]{1,0:T(8,128)S(1)} %multiply_reduce_fusion.6, f32[8,512]{1,0:T(8,128)S(1)} %multiply_reduce_fusion.7, bf16[8,512,64]{2,1,0:T(8,128)(2,1)} %gather_fusion.1, bf16[8,512,64]{2,1,0:T(8,128)(2,1)} %gather_fusion), kind=kOutput, calls=%fused_computation.20.clone.1 | convolution fusion | flops 278921216 | bytes 5275648 | tf_op jit(solution)/shard_map/while/body/eval_jaxpr/nom,nwm->now/dot_general | solution.py:30
  289.2 5.6 %exponential_convert_fusion.7 = bf16[8,512,512]{2,1,0:T(8,128)(2,1)} fusion(f32[8,512]{1,0:T(8,128)S(1)} %multiply_reduce_fusion.6, f32[8,512]{1,0:T(8,128)S(1)} %multiply_reduce_fusion.7, bf16[8,512,64]{2,1,0:T(8,128)(2,1)} %gather_fusion.1, bf16[8,512,64]{2,1,0:T(8,128)(2,1)} %gather_fusion), kind=kOutput, calls=%fused_computation.20.clone.1 | convolution fusion | flops 278921216 | bytes 5275648 | tf_op jit(solution)/shard_map/while/body/eval_jaxpr/nom,nwm->now/dot_general | solution.py:30
  316.7 5.6 %exponential_convert_fusion.7 = bf16[8,512,512]{2,1,0:T(8,128)(2,1)} fusion(f32[8,512]{1,0:T(8,128)S(1)} %multiply_reduce_fusion.6, f32[8,512]{1,0:T(8,128)S(1)} %multiply_reduce_fusion.7, bf16[8,512,64]{2,1,0:T(8,128)(2,1)} %gather_fusion.1, bf16[8,512,64]{2,1,0:T(8,128)(2,1)} %gather_fusion), kind=kOutput, calls=%fused_computation.20.clone.1 | convolution fusion | flops 278921216 | bytes 5275648 | tf_op jit(solution)/shard_map/while/body/eval_jaxpr/nom,nwm->now/dot_general | solution.py:30
  344.1 5.6 %exponential_convert_fusion.7 = bf16[8,512,512]{2,1,0:T(8,128)(2,1)} fusion(f32[8,512]{1,0:T(8,128)S(1)} %multiply_reduce_fusion.6, f32[8,512]{1,0:T(8,128)S(1)} %multiply_reduce_fusion.7, bf16[8,512,64]{2,1,0:T(8,128)(2,1)} %gather_fusion.1, bf16[8,512,64]{2,1,0:T(8,128)(2,1)} %gather_fusion), kind=kOutput, calls=%fused_computation.20.clone.1 | convolution fusion | flops 278921216 | bytes 5275648 | tf_op jit(solution)/shard_map/while/body/eval_jaxpr/nom,nwm->now/dot_general | solution.py:30
  371.5 5.6 %exponential_convert_fusion.7 = bf16[8,512,512]{2,1,0:T(8,128)(2,1)} fusion(f32[8,512]{1,0:T(8,128)S(1)} %multiply_reduce_fusion.6, f32[8,512]{1,0:T(8,128)S(1)} %multiply_reduce_fusion.7, bf16[8,512,64]{2,1,0:T(8,128)(2,1)} %gather_fusion.1, bf16[8,512,64]{2,1,0:T(8,128)(2,1)} %gather_fusion), kind=kOutput, calls=%fused_computation.20.clone.1 | convolution fusion | flops 278921216 | bytes 5275648 | tf_op jit(solution)/shard_map/while/body/eval_jaxpr/nom,nwm->now/dot_general | solution.py:30
  398.9 5.6 %exponential_convert_fusion.7 = bf16[8,512,512]{2,1,0:T(8,128)(2,1)} fusion(f32[8,512]{1,0:T(8,128)S(1)} %multiply_reduce_fusion.6, f32[8,512]{1,0:T(8,128)S(1)} %multiply_reduce_fusion.7, bf16[8,512,64]{2,1,0:T(8,128)(2,1)} %gather_fusion.1, bf16[8,512,64]{2,1,0:T(8,128)(2,1)} %gather_fusion), kind=kOutput, calls=%fused_computation.20.clone.1 | convolution fusion | flops 278921216 | bytes 5275648 | tf_op jit(solution)/shard_map/while/body/eval_jaxpr/nom,nwm->now/dot_general | solution.py:30
  426.4 5.6 %exponential_convert_fusion.7 = bf16[8,512,512]{2,1,0:T(8,128)(2,1)} fusion(f32[8,512]{1,0:T(8,128)S(1)} %multiply_reduce_fusion.6, f32[8,512]{1,0:T(8,128)S(1)} %multiply_reduce_fusion.7, bf16[8,512,64]{2,1,0:T(8,128)(2,1)} %gather_fusion.1, bf16[8,512,64]{2,1,0:T(8,128)(2,1)} %gather_fusion), kind=kOutput, calls=%fused_computation.20.clone.1 | convolution fusion | flops 278921216 | bytes 5275648 | tf_op jit(solution)/shard_map/while/body/eval_jaxpr/nom,nwm->now/dot_general | solution.py:30
  453.8 5.6 %exponential_convert_fusion.7 = bf16[8,512,512]{2,1,0:T(8,128)(2,1)} fusion(f32[8,512]{1,0:T(8,128)S(1)} %multiply_reduce_fusion.6, f32[8,512]{1,0:T(8,128)S(1)} %multiply_reduce_fusion.7, bf16[8,512,64]{2,1,0:T(8,128)(2,1)} %gather_fusion.1, bf16[8,512,64]{2,1,0:T(8,128)(2,1)} %gather_fusion), kind=kOutput, calls=%fused_computation.20.clone.1 | convolution fusion | flops 278921216 | bytes 5275648 | tf_op jit(solution)/shard_map/while/body/eval_jaxpr/nom,nwm->now/dot_general | solution.py:30
  481.2 5.6 %exponential_convert_fusion.7 = bf16[8,512,512]{2,1,0:T(8,128)(2,1)} fusion(f32[8,512]{1,0:T(8,128)S(1)} %multiply_reduce_fusion.6, f32[8,512]{1,0:T(8,128)S(1)} %multiply_reduce_fusion.7, bf16[8,512,64]{2,1,0:T(8,128)(2,1)} %gather_fusion.1, bf16[8,512,64]{2,1,0:T(8,128)(2,1)} %gather_fusion), kind=kOutput, calls=%fused_computation.20.clone.1 | convolution fusion | flops 278921216 | bytes 5275648 | tf_op jit(solution)/shard_map/while/body/eval_jaxpr/nom,nwm->now/dot_general | solution.py:30
  (241 shorter events, 295.2 us)
Async XLA Ops:
  0.0 39.8 %copy-start = (bf16[1,32,128,128]{3,2,1,0:T(8,128)(2,1)S(1)}, bf16[1,32,128,128]{3,2,1,0:T(8,128)(2,1)}, u32[]{:S(2)}) copy-start(bf16[1,32,128,128]{3,2,1,0:T(8,128)(2,1)} %param.21) | copy-start | bytes 3145732
  0.0 7.5 %copy-start.2 = (bf16[1,16384,64]{1,2,0:T(8,128)(2,1)S(1)}, bf16[1,16384,64]{1,2,0:T(8,128)(2,1)}, u32[]{:S(2)}) copy-start(bf16[1,16384,64]{1,2,0:T(8,128)(2,1)} %param.18) | copy-start | bytes 6291460
  2.1 1.5 copy-start.1
  3.6 7.1 %copy-start.8 = (s32[1,96,2]{1,2,0:T(2,128)S(1)}, s32[1,96,2]{1,2,0:T(2,128)}, u32[]{:S(2)}) copy-start(s32[1,96,2]{1,2,0:T(2,128)} %param.25) | copy-start | bytes 2308
  4.5 151.1 %collective-permute-start = (bf16[1,2048,80]{1,2,0:T(8,128)(2,1)}, bf16[1,2048,80]{1,2,0:T(8,128)(2,1)S(1)}, u32[]{:S(2)}, u32[]{:S(2)}) collective-permute-start(bf16[1,2048,80]{1,2,0:T(8,128)(2,1)} %get-tuple-element.247), channel_id=1, source_target_pairs={{0,4},{4,8},{8,12},{12,16},{16,20},{20,24},{24,28},{28,32},{32,36}... | collective-permute-start | bytes 983048 | tf_op jit(solution)/shard_map/ppermute | solution.py:19
  6.2 149.3 %collective-permute-start.1 = (bf16[1,2048,80]{1,2,0:T(8,128)(2,1)}, bf16[1,2048,80]{1,2,0:T(8,128)(2,1)}, u32[]{:S(2)}, u32[]{:S(2)}) collective-permute-start(bf16[1,2048,80]{1,2,0:T(8,128)(2,1)} %get-tuple-element.248), channel_id=1, source_target_pairs={{4,0},{8,4},{12,8},{16,12},{20,16},{24,20},{28,24},{32,28},{36,32}... | collective-permute-start | bytes 983048 | tf_op jit(solution)/shard_map/ppermute | solution.py:22
  38.2 34.8 %copy-start.10 = (s32[1,6]{1,0:T(1,128)S(1)}, s32[1,6]{1,0:T(1,128)}, u32[]{:S(2)}) copy-start(s32[1,6]{1,0:T(1,128)} %param.27) | copy-start | bytes 76
  38.2 34.8 %copy-start.7 = (bf16[1,1,128,128]{3,2,1,0:T(8,128)(2,1)S(1)}, bf16[1,1,128,128]{3,2,1,0:T(8,128)(2,1)}, u32[]{:S(2)}) copy-start(bf16[1,1,128,128]{3,2,1,0:T(8,128)(2,1)} %param.22) | copy-start | bytes 98308
  38.2 112.2 %copy-start.9 = (bf16[1,4,128,128]{3,2,1,0:T(8,128)(2,1)S(1)}, bf16[1,4,128,128]{3,2,1,0:T(8,128)(2,1)}, u32[]{:S(2)}) copy-start(bf16[1,4,128,128]{3,2,1,0:T(8,128)(2,1)} %param.24) | copy-start | bytes 393220
  39.8 110.5 %copy-start.6 = (bf16[1,6,128,128]{3,2,1,0:T(8,128)(2,1)S(1)}, bf16[1,6,128,128]{3,2,1,0:T(8,128)(2,1)}, u32[]{:S(2)}) copy-start(bf16[1,6,128,128]{3,2,1,0:T(8,128)(2,1)} %param.23) | copy-start | bytes 589828
  496.6 3.0 copy-start.4
  496.7 5.0 copy-start.3
  496.7 4.9 copy-start.5
  496.7 3.1 collective-permute-start.2
  498.4 3.2 collective-permute-start.3
where the time goes:
time: 509 us; the launch traced here: 503 us
  matrix products  167 us (33%)
  local copies, waits for them, and re-layouts  134 us (26%)
  blocking collectives  106 us (21%)
  other arithmetic  86.6 us (17%)
  starting transfers between devices  5.76 us (1%)
    dot_general x12, matrix products, kernel_tiles(): jnp.einsum('nom,nwm->now', left_samples, right_samples, preferred_element...  66.7 us
    psum x1, blocking collectives, on_device(): group_total = lax.psum(group_term, 'inner')  66.3 us
    gather x12, local copies, waits for them, and re-layouts, one_block(): widened_points[second_slot]  49.8 us
    gather x12, local copies, waits for them, and re-layouts, one_block(): widened_points[first_slot]  49.8 us
    dot_general x12, matrix products, one_block(): jnp.einsum('bpq,bqn->bpn', kernel, widened_charges[second_slot], preferre...  40.5 us
    dot_general x12, matrix products, one_block(): jnp.einsum('bpq,bpn->bqn', kernel, widened_charges[first_slot], preferred...  33.9 us
    all_gather x1, blocking collectives, on_device(): all_nodes = lax.all_gather(node_skeleton[None], 'inner', axis=0, tiled=True)  29.9 us
    reduce_sum x16, other arithmetic, kernel_tiles(): left_square = jnp.sum(jnp.square(left_samples.astype(jnp.float32)), -1)  29.4 us
  transfers between devices with their start and end apart: 4, of which 1 were waited for; matrix products, arithmetic and copies ran while one was open for 8% of the time, Pallas kernels for 0%

commit v1 on v0

v1 whole, which is shorter than its diff:
```python
import functools

import jax
import jax.numpy as jnp
from jax import lax
from jax.experimental import pallas as pl
from jax.experimental.pallas import tpu as pltpu
from jax.sharding import PartitionSpec as P

REACH = 4
RIDGE = 0.25
BF = jnp.bfloat16
F32 = jnp.float32
DEPTH = 128
VMEM = pl.BlockSpec(memory_space=pltpu.VMEM)
SMEM = pl.BlockSpec(memory_space=pltpu.SMEM)
PARAMS = pltpu.CompilerParams(vmem_limit_bytes=56 * 2**20)


def dot(left, right, left_dim, right_dim):
    return lax.dot_general(
        left, right, (((left_dim,), (right_dim,)), ((), ())), preferred_element_type=F32
    )


def half_square(block):
    wide = block.astype(F32)
    total = 0.5 * jnp.sum(wide * wide, 0, keepdims=True)
    high = total.astype(BF).astype(F32)
    rest = total - high
    middle = rest.astype(BF).astype(F32)
    low = rest - middle
    return high, middle, low


def augment(block, first):
    dim, count = block.shape
    parts = half_square(block)
    row = lax.broadcasted_iota(jnp.int32, (DEPTH - dim, count), 0)
    at = 0 if first else 3
    extra = jnp.where((row >= 3 - at) & (row < 6 - at), 1.0, 0.0)
    for k in range(3):
        extra = jnp.where(row == at + k, -parts[k], extra)
    return jnp.concatenate([block, extra.astype(BF)], 0)


def skeleton_kernel(bases, charges, transfers, parent, node, term):
    leaves, leaf, _ = bases.shape

    def step(index, total):
        cols = pl.ds(pl.multiple_of(index * leaf, leaf), leaf)
        skeleton = dot(charges[:, cols], bases[index], 1, 0).astype(BF)
        return total + dot(skeleton, transfers[index], 1, 0)

    total = lax.fori_loop(
        0, leaves, step, jnp.zeros((charges.shape[0], transfers.shape[2]), F32), unroll=4
    )
    node[...] = total.astype(BF)
    term[...] = dot(total.astype(BF), parent[...], 1, 0)


def split_pairs(pairs, count, halo_list, own_list, leaves):
    def step(index, counts):
        halo_count, own_count = counts
        first, second = pairs[0, index], pairs[1, index]
        own = ((second >= REACH) & (second < REACH + leaves)).astype(jnp.int32)
        code = first * 64 + second
        halo_list[halo_count] = code
        own_list[own_count] = code
        return halo_count + 1 - own, own_count + own

    return lax.fori_loop(0, count, step, (jnp.int32(0), jnp.int32(0)))


def grouped(count, body, group):
    def block(index, carry):
        for k in range(group):
            body(index * group + k)
        return carry

    whole = count // group
    lax.fori_loop(0, whole, block, 0)

    def single(index, carry):
        body(index)
        return carry

    lax.fori_loop(whole * group, count, single, 0)


def halo_kernel(
    pairs, live, points, charges, halo_points, halo_charges,
    first_out, totals, halo_totals,
    second, halo_list, own_list,
):
    leaves, leaf, _ = first_out.shape
    totals[...] = jnp.zeros_like(totals)
    halo_totals[...] = jnp.zeros_like(halo_totals)

    def build(index, carry):
        cols = pl.ds(pl.multiple_of(index * leaf, leaf), leaf)
        first_out[index] = augment(points[:, cols], True).T
        return carry

    lax.fori_loop(0, leaves, build, 0)

    def build_halo(index, carry):
        cols = pl.ds(pl.multiple_of(index * leaf, leaf), leaf)
        second[index] = augment(halo_points[:, cols], False)
        return carry

    lax.fori_loop(0, 2 * REACH, build_halo, 0)
    halo_count, _ = split_pairs(pairs, live[0, 0], halo_list, own_list, leaves)

    def body(index):
        code = halo_list[index]
        a, b = code // 64, code % 64
        b = jnp.where(b < REACH, b, b - leaves)
        cols_a = pl.ds(pl.multiple_of(a * leaf, leaf), leaf)
        cols_b = pl.ds(pl.multiple_of(b * leaf, leaf), leaf)
        tile = jnp.exp(dot(first_out[a], second[b], 1, 0)).astype(BF)
        halo_totals[:, cols_b] += dot(charges[:, cols_a], tile, 1, 0)
        totals[:, cols_a] += dot(halo_charges[:, cols_b], tile, 1, 1)

    grouped(halo_count, body, 4)


def own_kernel(
    pairs, live, points, charges, first, start,
    totals,
    second, halo_list, own_list,
):
    leaves, leaf, _ = first.shape

    def build(index, carry):
        cols = pl.ds(pl.multiple_of(index * leaf, leaf), leaf)
        second[index] = augment(points[:, cols], False)
        return carry

    lax.fori_loop(0, leaves, build, 0)

    def diagonal(index, carry):
        cols = pl.ds(pl.multiple_of(index * leaf, leaf), leaf)
        tile = jnp.exp(dot(first[index], second[index], 1, 0)).astype(BF)
        own = charges[:, cols]
        totals[:, cols] = start[:, cols] + RIDGE * own.astype(F32) + dot(own, tile, 1, 0)
        return carry

    lax.fori_loop(0, leaves, diagonal, 0, unroll=4)
    _, own_count = split_pairs(pairs, live[0, 0], halo_list, own_list, leaves)

    def body(index):
        code = own_list[index]
        a, b = code // 64, code % 64 - REACH
        cols_a = pl.ds(pl.multiple_of(a * leaf, leaf), leaf)
        cols_b = pl.ds(pl.multiple_of(b * leaf, leaf), leaf)
        tile = jnp.exp(dot(first[a], second[b], 1, 0)).astype(BF)
        totals[:, cols_b] += dot(charges[:, cols_a], tile, 1, 0)
        totals[:, cols_a] += dot(charges[:, cols_b], tile, 1, 1)

    grouped(own_count, body, 4)


def finish_kernel(
    bases, transfers, parent, couplings, group_couplings, nodes, groups, far, weight, near, low, high,
    out,
):
    leaves, leaf, _ = bases.shape
    group_field = sum(
        dot(groups[h], group_couplings[h] * weight[h].astype(BF), 1, 1)
        for h in range(groups.shape[0])
    ).astype(BF)
    field = dot(group_field, parent[...], 1, 1)
    for j in range(couplings.shape[0]):
        field += dot(nodes[far[0, j]], couplings[j], 1, 1)
    field = field.astype(BF)
    rim = REACH * leaf

    def step(index, carry):
        cols = pl.ds(pl.multiple_of(index * leaf, leaf), leaf)
        leaf_field = dot(field, transfers[index], 1, 1).astype(BF)
        out[:, cols] = near[:, cols] + dot(leaf_field, bases[index], 1, 1)
        return carry

    lax.fori_loop(0, leaves, step, 0, unroll=4)
    out[:, :rim] += low[...]
    out[:, out.shape[1] - rim :] += high[...]


def on_device(
    points, charges, bases, transfers, parents, couplings, group_couplings, near_pairs, pair_count, far_list
):
    leaves = transfers.shape[1]
    count = points.shape[1]
    leaf = count // leaves
    dim, rhs, rank = points.shape[2], charges.shape[2], bases.shape[2]
    slots = near_pairs.shape[1]
    rim = REACH * leaf
    pt = jnp.swapaxes(points[0], 0, 1)
    ct = jnp.swapaxes(charges[0], 0, 1)
    pairs = jnp.swapaxes(near_pairs[0], 0, 1)
    size = lax.axis_size("inner")
    forward = [(i, i + 1) for i in range(size - 1)]
    backward = [(i + 1, i) for i in range(size - 1)]

    joined = jnp.concatenate([pt, ct], 0)
    low = lax.ppermute(joined[:, count - rim :], "inner", forward)
    high = lax.ppermute(joined[:, :rim], "inner", backward)

    leaf_bases = bases[0].reshape(leaves, leaf, rank)
    node, term = pl.pallas_call(
        skeleton_kernel,
        out_shape=[
            jax.ShapeDtypeStruct((rhs, rank), BF),
            jax.ShapeDtypeStruct((rhs, rank), F32),
        ],
        in_specs=[VMEM] * 4,
        out_specs=[VMEM] * 2,
        compiler_params=PARAMS,
        cost_estimate=pl.CostEstimate(flops=10**9, bytes_accessed=6 * 2**20, transcendentals=0),
        name="skeleton",
    )(leaf_bases, ct, transfers[0], parents[0, 0])
    all_nodes = lax.all_gather(node[None], "inner", axis=0, tiled=True)
    group_total = lax.psum(term, "inner").astype(BF)
    groups = lax.all_gather(group_total[None], "outer", axis=0, tiled=True)

    halo = jnp.concatenate([low, high], 1)
    lists = [pltpu.SMEM((slots + 1,), jnp.int32)] * 2
    first, totals, halo_totals = pl.pallas_call(
        halo_kernel,
        out_shape=[
            jax.ShapeDtypeStruct((leaves, leaf, DEPTH), BF),
            jax.ShapeDtypeStruct((rhs, count), F32),
            jax.ShapeDtypeStruct((rhs, 2 * rim), F32),
        ],
        in_specs=[SMEM, SMEM] + [VMEM] * 4,
        out_specs=[VMEM] * 3,
        scratch_shapes=[pltpu.VMEM((2 * REACH, DEPTH, leaf), BF)] + lists,
        compiler_params=PARAMS,
        cost_estimate=pl.CostEstimate(
            flops=64 * 10**9, bytes_accessed=8 * 2**20, transcendentals=64 * leaf * leaf
        ),
        name="halo_pairs",
    )(pairs, pair_count, pt, ct, halo[:dim], halo[dim:])
    back_low = lax.ppermute(halo_totals[:, rim:], "inner", forward)
    back_high = lax.ppermute(halo_totals[:, :rim], "inner", backward)
    near = pl.pallas_call(
        own_kernel,
        out_shape=jax.ShapeDtypeStruct((rhs, count), F32),
        in_specs=[SMEM, SMEM] + [VMEM] * 4,
        out_specs=VMEM,
        scratch_shapes=[pltpu.VMEM((leaves, DEPTH, leaf), BF)] + lists,
        compiler_params=PARAMS,
        cost_estimate=pl.CostEstimate(
            flops=64 * 10**9, bytes_accessed=8 * 2**20, transcendentals=64 * leaf * leaf
        ),
        name="own_pairs",
    )(pairs, pair_count, pt, ct, first, totals)
    own_group = lax.axis_index("outer")
    weight = (jnp.arange(lax.axis_size("outer"), dtype=jnp.int32) != own_group).astype(F32)
    out = pl.pallas_call(
        finish_kernel,
        out_shape=jax.ShapeDtypeStruct((rhs, count), F32),
        in_specs=[VMEM] * 7 + [SMEM, SMEM] + [VMEM] * 3,
        out_specs=VMEM,
        compiler_params=PARAMS,
        cost_estimate=pl.CostEstimate(flops=10**9, bytes_accessed=8 * 2**20, transcendentals=0),
        name="finish",
    )(
        leaf_bases, transfers[0], parents[0, 0], couplings[0], group_couplings[0],
        all_nodes, groups, far_list, weight, near, back_low, back_high,
    )
    return jnp.swapaxes(out, 0, 1)[None]


def solution(mesh):
    placed = (
        P("outer", "inner", None),
        P("outer", "inner", None),
        P("outer", "inner", None),
        P("outer", "inner", None, None),
        P("outer", "inner", None, None),
        P("outer", "inner", None, None),
        P("outer", None, None, None),
        P("outer", "inner", None),
        P("outer", "inner"),
        P("outer", "inner"),
    )
    return jax.shard_map(
        on_device, mesh=mesh, in_specs=placed, out_specs=P("outer", "inner", None), check_vma=False
    )
```

time: 509 us -> 209 us (0.41)
  the two profiles are of different devices: /device:TPU:16 before, /device:TPU:58 now
where the time goes in v1:
time: 209 us
  blocking collectives  103 us (49%)
  Pallas kernels  84.8 us (41%)
  starting transfers between devices  15.6 us (7%)
  local copies, waits for them, and re-layouts  3.21 us (2%)
    psum x1, blocking collectives, on_device(): group_total = lax.psum(term, 'inner').astype(BF)  52.4 us
    all_gather x1, blocking collectives, on_device(): all_nodes = lax.all_gather(node[None], 'inner', axis=0, tiled=True)  38.2 us
    pallas_call x1, Pallas kernels, on_device(): pl.pallas_call(halo_kernel, out_shape=[jax.ShapeDtypeStruct((leaves, leaf...  35 us
    pallas_call x1, Pallas kernels, on_device(): pl.pallas_call(own_kernel, out_shape=jax.ShapeDtypeStruct((rhs, count), F...  31.7 us
    all_gather x1, blocking collectives, on_device(): groups = lax.all_gather(group_total[None], 'outer', axis=0, tiled=True)  12.5 us
    pallas_call x1, Pallas kernels, on_device(): pl.pallas_call(finish_kernel, out_shape=jax.ShapeDtypeStruct((rhs, count)...  10.2 us
    pallas_call x1, Pallas kernels, on_device(): pl.pallas_call(skeleton_kernel, out_shape=[jax.ShapeDtypeStruct((rhs, ran...  7.84 us
    ppermute x1, starting transfers between devices, on_device(): back_high = lax.ppermute(halo_totals[:, :rim], 'inner', backward)  6.53 us
  transfers between devices with their start and end apart: 4, of which 0 were waited for; matrix products, arithmetic and copies ran while one was open for 0% of the time, Pallas kernels for 19%

profile of v1, /device:TPU:58, one launch (start us, length us, event | category | flops | bytes accessed | tf_op | source)
XLA Modules:
  0.0 209.2 jit_solution(17513271731023275792)
XLA Ops:
  0.0 1.2 pad_maximum_fusion
  1.2 1.9 collective-permute-start
  3.1 3.6 %collective-permute-start.1 = (bf16[80,2048]{1,0:T(8,128)(2,1)S(1)}, bf16[80,2048]{1,0:T(8,128)(2,1)S(1)}, u32[]{:S(2)}, u32[]{:S(2)}) collective-permute-start(bf16[80,2048]{1,0:T(8,128)(2,1)S(1)} %get-tuple-element.15), channel_id=1, source_target_pairs={{4,0},{8,4},{12,8},{16,12},{20,16},{24,20},{28,24},{32,28},{36,32}... | collective-permute-start | bytes 983048 | tf_op jit(solution)/shard_map/ppermute | solution.py:208
  7.4 7.8 %skeleton.1 = (bf16[16,128]{1,0:T(8,128)(2,1)}, f32[16,128]{1,0:T(8,128)}) custom-call(bf16[32,512,128]{2,1,0:T(8,128)(2,1)} %bitcast.19, bf16[16,16384]{1,0:T(8,128)(2,1)} %bitcast.27, bf16[32,128,128]{2,1,0:T(8,128)(2,1)} %bitcast.21, bf16[128,128]{1,0:T(8,128)(2,1)} %bitcast.33), custom_call_target="tpu_custom_call" | custom-call | flops 1000000000 | bytes 6291456 | tf_op jit(solution)/shard_map/skeleton/pallas_call | solution.py:211
  15.2 52.4 %psum.7 = bf16[16,128]{1,0:T(8,128)(2,1)S(1)} all-reduce(f32[16,128]{1,0:T(8,128)} %get-tuple-element.11), channel_id=1, replica_groups=mesh['inner'=32,'outer'=4] {'inner'}, use_global_device_ids=true, to_apply=%region_0.0 | all-reduce | flops 2048 | bytes 12288 | tf_op jit(solution)/shard_map/psum | solution.py:224
  67.6 12.5 %all-gather.1 = bf16[64,128]{1,0:T(8,128)(2,1)} all-gather(bf16[16,128]{1,0:T(8,128)(2,1)S(1)} %psum.7), channel_id=3, replica_groups=mesh['inner'=32,'outer'=4] {'outer'}, dimensions={0}, use_global_device_ids=true | all-gather | bytes 20480 | tf_op jit(solution)/shard_map/all_gather | solution.py:225
  80.1 38.2 %all-gather = bf16[512,128]{1,0:T(8,128)(2,1)} all-gather(bf16[16,128]{1,0:T(8,128)(2,1)} %get-tuple-element.10), channel_id=2, replica_groups=mesh['inner'=32,'outer'=4] {'inner'}, dimensions={0}, use_global_device_ids=true | all-gather | bytes 135168 | tf_op jit(solution)/shard_map/all_gather | solution.py:223
  118.3 0.6 compare_convert_fusion.weight
  118.9 0.0 collective-permute-done
  118.9 0.0 collective-permute-done.1
  119.0 0.8 slice.24.halo_points
  119.8 0.7 slice.25.halo_charges
  120.5 35.0 %halo_pairs.1 = (bf16[32,512,128]{2,1,0:T(8,128)(2,1)}, f32[16,16384]{1,0:T(8,128)}, f32[16,4096]{1,0:T(8,128)}) custom-call(s32[2,96]{1,0:T(2,128)} %bitcast.36, s32[1,1]{1,0:T(1,128)S(6)} %copy.12.live, bf16[64,16384]{1,0:T(8,128)(2,1)} %bitcast.24, bf16[16,16384]{1,0:T(8,128)(2,1)} %bitcast.28, bf16[64,4096]{1,0:T(8,128)(2,1)} %slice.24.halo_points, ...), custom_call_target="tpu_custom_call" | custom-call | flops 64000000000 | bytes 8388608 | tf_op jit(solution)/shard_map/halo_pairs/pallas_call | solution.py:229
  155.5 1.0 fusion
  156.5 3.5 %collective-permute-start.2 = (f32[16,2048]{1,0:T(8,128)S(1)}, f32[16,2048]{1,0:T(8,128)S(1)}, u32[]{:S(2)}, u32[]{:S(2)}) collective-permute-start(f32[16,2048]{1,0:T(8,128)S(1)} %get-tuple-element.18), channel_id=1, source_target_pairs={{0,4},{4,8},{8,12},{12,16},{16,20},{20,24},{24,28},{28,32},{32,36}... | collective-permute-start | bytes 393224 | tf_op jit(solution)/shard_map/ppermute | solution.py:245
  160.0 6.5 %collective-permute-start.3 = (f32[16,2048]{1,0:T(8,128)S(1)}, f32[16,2048]{1,0:T(8,128)S(1)}, u32[]{:S(2)}, u32[]{:S(2)}) collective-permute-start(f32[16,2048]{1,0:T(8,128)S(1)} %get-tuple-element.17), channel_id=1, source_target_pairs={{4,0},{8,4},{12,8},{16,12},{20,16},{24,20},{28,24},{32,28},{36,32}... | collective-permute-start | bytes 393224 | tf_op jit(solution)/shard_map/ppermute | solution.py:246
  166.5 31.7 %own_pairs.1.near = f32[16,16384]{1,0:T(8,128)} custom-call(s32[2,96]{1,0:T(2,128)} %bitcast.37, s32[1,1]{1,0:T(1,128)S(6)} %copy.12.live, bf16[64,16384]{1,0:T(8,128)(2,1)} %bitcast.25, bf16[16,16384]{1,0:T(8,128)(2,1)} %bitcast.29, bf16[32,512,128]{2,1,0:T(8,128)(2,1)} %get-tuple-element.12.first, f32[16,16384]{1,0:T(8,128)} %get-tuple-element.13.start), custom_call_target="tpu_custom_call" | custom-call | flops 64000000000 | bytes 8388608 | tf_op jit(solution)/shard_map/own_pairs/pallas_call | solution.py:247
  198.2 0.0 collective-permute-done.2.low
  198.2 0.0 copy-start
  198.2 0.0 collective-permute-done.3.high
  198.2 0.0 copy-start.1
  198.2 0.6 copy-done
  198.9 0.0 copy-done.1
  198.9 10.2 %finish.1 = f32[16,16384]{1,0:T(8,128)} custom-call(bf16[32,512,128]{2,1,0:T(8,128)(2,1)} %bitcast.20, bf16[32,128,128]{2,1,0:T(8,128)(2,1)} %bitcast.22, bf16[128,128]{1,0:T(8,128)(2,1)} %bitcast.34, bf16[6,128,128]{2,1,0:T(8,128)(2,1)} %bitcast.31, bf16[4,128,128]{2,1,0:T(8,128)(2,1)} %bitcast.32, bf16[32,16,128]{2,1,0:T(8,128)(2,1)} %bitcast.30, ...), custom_call_target="tpu_custom_call" | custom-call | flops 1000000000 | bytes 8388608 | tf_op jit(solution)/shard_map/finish/pallas_call | solution.py:261
  (2 shorter events, 0.0 us)
Async XLA Ops:
  1.2 117.7 %collective-permute-start = (bf16[80,2048]{1,0:T(8,128)(2,1)S(1)}, bf16[80,2048]{1,0:T(8,128)(2,1)S(1)}, u32[]{:S(2)}, u32[]{:S(2)}) collective-permute-start(bf16[80,2048]{1,0:T(8,128)(2,1)S(1)} %get-tuple-element.16), channel_id=1, source_target_pairs={{0,4},{4,8},{8,12},{12,16},{16,20},{20,24},{24,28},{28,32},{32,36}... | collective-permute-start | bytes 983048 | tf_op jit(solution)/shard_map/ppermute | solution.py:207
  3.1 115.8 %collective-permute-start.1 = (bf16[80,2048]{1,0:T(8,128)(2,1)S(1)}, bf16[80,2048]{1,0:T(8,128)(2,1)S(1)}, u32[]{:S(2)}, u32[]{:S(2)}) collective-permute-start(bf16[80,2048]{1,0:T(8,128)(2,1)S(1)} %get-tuple-element.15), channel_id=1, source_target_pairs={{4,0},{8,4},{12,8},{16,12},{20,16},{24,20},{28,24},{32,28},{36,32}... | collective-permute-start | bytes 983048 | tf_op jit(solution)/shard_map/ppermute | solution.py:208
  156.5 41.7 %collective-permute-start.2 = (f32[16,2048]{1,0:T(8,128)S(1)}, f32[16,2048]{1,0:T(8,128)S(1)}, u32[]{:S(2)}, u32[]{:S(2)}) collective-permute-start(f32[16,2048]{1,0:T(8,128)S(1)} %get-tuple-element.18), channel_id=1, source_target_pairs={{0,4},{4,8},{8,12},{12,16},{16,20},{20,24},{24,28},{28,32},{32,36}... | collective-permute-start | bytes 393224 | tf_op jit(solution)/shard_map/ppermute | solution.py:245
  160.0 38.2 %collective-permute-start.3 = (f32[16,2048]{1,0:T(8,128)S(1)}, f32[16,2048]{1,0:T(8,128)S(1)}, u32[]{:S(2)}, u32[]{:S(2)}) collective-permute-start(f32[16,2048]{1,0:T(8,128)S(1)} %get-tuple-element.17), channel_id=1, source_target_pairs={{4,0},{8,4},{12,8},{16,12},{20,16},{24,20},{28,24},{32,28},{36,32}... | collective-permute-start | bytes 393224 | tf_op jit(solution)/shard_map/ppermute | solution.py:246
  198.2 0.7 copy-start
  198.2 0.7 copy-start.1

commit v2 on v0

v2 whole, which is shorter than its diff:
```python
import functools

import jax
import jax.numpy as jnp
from jax import lax
from jax.experimental import pallas as pl
from jax.experimental.pallas import tpu as pltpu
from jax.sharding import PartitionSpec as P

REACH = 4
RIDGE = 0.25
EXTRA = 16
GROUP = 4
BF = jnp.bfloat16
F32 = jnp.float32
VMEM = pl.BlockSpec(memory_space=pltpu.VMEM)
SMEM = pl.BlockSpec(memory_space=pltpu.SMEM)
ANY = pl.BlockSpec(memory_space=pl.ANY)
MESH = pl.DeviceIdType.MESH
LIMIT = 56 * 2**20


def dot(left, right, left_dim, right_dim):
    return lax.dot_general(
        left, right, (((left_dim,), (right_dim,)), ((), ())), preferred_element_type=F32
    )


def norm_rows(block):
    wide = block.astype(F32)
    total = 0.5 * jnp.sum(wide * wide, 0, keepdims=True)
    high = total.astype(BF).astype(F32)
    rest = total - high
    middle = rest.astype(BF).astype(F32)
    parts = (high, middle, rest - middle)
    row = lax.broadcasted_iota(jnp.int32, (EXTRA, block.shape[1]), 0)
    first = jnp.where((row >= 3) & (row < 6), 1.0, 0.0)
    second = jnp.where(row < 3, 1.0, 0.0)
    for k in range(3):
        first = jnp.where(row == k, -parts[k], first)
        second = jnp.where(row == 3 + k, -parts[k], second)
    return first.astype(BF), second.astype(BF)


def columns(index, width):
    return pl.ds(pl.multiple_of(index * width, width), width)


def tile_of(points, firsts, seconds, cols_a, cols_b):
    left = jnp.concatenate([points[:, cols_a], firsts[:, cols_a]], 0)
    right = jnp.concatenate([points[:, cols_b], seconds[:, cols_b]], 0)
    return jnp.exp(dot(left, right, 0, 0)).astype(BF)


def exchange_kernel(
    inner, outer, leaves,
    pt_hbm, ct_hbm, bases_hbm, transfers_hbm, parent, couplings, group_couplings, far,
    halo_points, halo_charges, near, field_out,
    points, charges, bases, transfers, skeletons, packed, slots, group_slots,
    load_sem, halo_send, halo_recv, node_send, node_recv, group_send, group_recv,
):
    me, group = lax.axis_index("inner"), lax.axis_index("outer")
    right, left = lax.rem(me + 1, inner), lax.rem(me + inner - 1, inner)
    rhs, count = ct_hbm.shape
    leaf = count // leaves
    rim = REACH * leaf
    rank = parent.shape[1]
    chunk = 8
    loads = [
        pltpu.make_async_copy(ct_hbm, charges, load_sem.at[0]),
        pltpu.make_async_copy(transfers_hbm, transfers, load_sem.at[1]),
        pltpu.make_async_copy(pt_hbm, points, load_sem.at[2]),
    ]
    base_loads = [
        pltpu.make_async_copy(
            bases_hbm.at[pl.ds(k * chunk, chunk)], bases.at[pl.ds(k * chunk, chunk)], load_sem.at[3 + k]
        )
        for k in range(leaves // chunk)
    ]
    loads[0].start()
    for copy in base_loads:
        copy.start()
    loads[1].start()
    loads[2].start()
    barrier = pltpu.get_barrier_semaphore()
    for k in range(1, inner):
        pl.semaphore_signal(
            barrier, inc=1, device_id={"inner": lax.rem(me + k, inner)}, device_id_type=MESH
        )
    for k in range(1, outer):
        pl.semaphore_signal(
            barrier, inc=1, device_id={"outer": lax.rem(group + k, outer)}, device_id_type=MESH
        )

    loads[0].wait()
    for k, copy in enumerate(base_loads):
        copy.wait()
        for index in range(k * chunk, (k + 1) * chunk):
            block = charges[:, index * leaf : (index + 1) * leaf]
            skeletons[:, index * rank : (index + 1) * rank] = dot(block, bases[index], 1, 0).astype(BF)
    loads[1].wait()
    node = dot(skeletons[...], transfers[...], 1, 0).astype(BF)
    packed[:rhs] = node.astype(F32)
    packed[rhs:] = dot(node, parent[...], 1, 0)
    slots[me] = packed[...]

    pl.semaphore_wait(barrier, inner + outer - 2)

    def node_copy(k):
        return pltpu.make_async_remote_copy(
            src_ref=packed, dst_ref=slots.at[me], send_sem=node_send.at[k], recv_sem=node_recv.at[me],
            device_id={"inner": lax.rem(me + k, inner)}, device_id_type=MESH,
        )

    for k in range(1, inner):
        node_copy(k).start()
    halo_copies = []
    for k, (source, target, peer, begin) in enumerate((
        (pt_hbm, halo_points.at[0], right, count - rim),
        (ct_hbm, halo_charges.at[0], right, count - rim),
        (pt_hbm, halo_points.at[1], left, 0),
        (ct_hbm, halo_charges.at[1], left, 0),
    )):
        copy = pltpu.make_async_remote_copy(
            src_ref=source.at[:, pl.ds(begin, rim)], dst_ref=target,
            send_sem=halo_send.at[k], recv_sem=halo_recv.at[k],
            device_id={"inner": peer}, device_id_type=MESH,
        )
        copy.start()
        halo_copies.append(copy)
    loads[2].wait()

    def diagonal(index, carry):
        cols = columns(index, leaf)
        first, second = norm_rows(points[:, cols])
        left_form = jnp.concatenate([points[:, cols], first], 0)
        right_form = jnp.concatenate([points[:, cols], second], 0)
        tile = jnp.exp(dot(left_form, right_form, 0, 0)).astype(BF)
        own = charges[:, cols]
        near[:, cols] = RIDGE * own.astype(F32) + dot(own, tile, 1, 0)
        return carry

    half = leaves // 2
    lax.fori_loop(0, half, diagonal, 0, unroll=4)

    for k in range(1, inner):
        sender = lax.rem(me + k, inner)
        pltpu.make_async_copy(packed, slots.at[sender], node_recv.at[sender]).wait()
    group_slots[group] = jnp.sum(slots[:, rhs:], 0).astype(BF)

    def group_copy(k):
        return pltpu.make_async_remote_copy(
            src_ref=group_slots.at[group], dst_ref=group_slots.at[group],
            send_sem=group_send.at[k], recv_sem=group_recv.at[group],
            device_id={"outer": lax.rem(group + k, outer)}, device_id_type=MESH,
        )

    for k in range(1, outer):
        group_copy(k).start()
    field = jnp.zeros((rhs, rank), F32)
    for j in range(couplings.shape[0]):
        field += dot(slots[far[0, j], :rhs].astype(BF), couplings[j], 1, 1)
    lax.fori_loop(half, leaves, diagonal, 0, unroll=4)
    group_field = jnp.zeros((rhs, rank), F32)
    for k in range(1, outer):
        sender = lax.rem(group + k, outer)
        pltpu.make_async_copy(group_slots.at[group], group_slots.at[sender], group_recv.at[sender]).wait()
        group_field += dot(group_slots[sender], group_couplings[sender], 1, 1)
    field += dot(group_field.astype(BF), parent[...], 1, 1)
    field_out[...] = field.astype(BF)
    for k in range(1, inner):
        node_copy(k).wait_send()
    for k in range(1, outer):
        group_copy(k).wait_send()
    for copy in halo_copies:
        copy.wait()


def pair_kernel(
    leaves, leaf,
    pairs, live, pt_hbm, ct_hbm, halo_points, halo_charges, near_hbm,
    out_near, out_halo,
    points, charges, firsts, seconds, totals, sem,
):
    rim = REACH * leaf
    count = leaves * leaf
    spots = (pl.ds(0, rim), pl.ds(rim + count, rim))
    own = pl.ds(rim, count)
    copies = [
        pltpu.make_async_copy(pt_hbm, points.at[:, own], sem.at[0]),
        pltpu.make_async_copy(halo_points.at[0], points.at[:, spots[0]], sem.at[1]),
        pltpu.make_async_copy(halo_points.at[1], points.at[:, spots[1]], sem.at[2]),
        pltpu.make_async_copy(ct_hbm, charges.at[:, own], sem.at[3]),
        pltpu.make_async_copy(halo_charges.at[0], charges.at[:, spots[0]], sem.at[4]),
        pltpu.make_async_copy(halo_charges.at[1], charges.at[:, spots[1]], sem.at[5]),
        pltpu.make_async_copy(near_hbm, totals.at[:, own], sem.at[6]),
    ]
    for copy in copies:
        copy.start()
    for spot in spots:
        totals[:, spot] = jnp.zeros((totals.shape[0], rim), F32)
    for copy in copies:
        copy.wait()

    def build(index, carry):
        cols = columns(index, leaf)
        firsts[:, cols], seconds[:, cols] = norm_rows(points[:, cols])
        return carry

    lax.fori_loop(0, leaves + 2 * REACH, build, 0, unroll=2)

    def body(index):
        cols_a = columns(pairs[0, index] + REACH, leaf)
        cols_b = columns(pairs[1, index], leaf)
        tile = tile_of(points, firsts, seconds, cols_a, cols_b)
        totals[:, cols_b] += dot(charges[:, cols_a], tile, 1, 0)
        totals[:, cols_a] += dot(charges[:, cols_b], tile, 1, 1)

    def block(index, carry):
        for k in range(GROUP):
            body(index * GROUP + k)
        return carry

    def single(index, carry):
        body(index)
        return carry

    number = live[0, 0]
    whole = number // GROUP
    lax.fori_loop(0, whole, block, 0)
    lax.fori_loop(whole * GROUP, number, single, 0)
    writes = [
        pltpu.make_async_copy(totals.at[:, own], out_near, sem.at[0]),
        pltpu.make_async_copy(totals.at[:, spots[0]], out_halo.at[0], sem.at[1]),
        pltpu.make_async_copy(totals.at[:, spots[1]], out_halo.at[1], sem.at[2]),
    ]
    for copy in writes:
        copy.start()
    for copy in writes:
        copy.wait()


def finish_kernel(
    inner,
    halo, near_hbm, bases_hbm, transfers_hbm, field,
    out,
    near, bases, transfers, leaf_fields, arrived, load_sem, send_sem, recv_sem,
):
    me = lax.axis_index("inner")
    right, left = lax.rem(me + 1, inner), lax.rem(me + inner - 1, inner)
    leaves, leaf, rank = bases.shape
    count = near.shape[1]
    rim = REACH * leaf
    chunk = 8
    barrier = pltpu.get_barrier_semaphore()
    for peer in (left, right):
        pl.semaphore_signal(barrier, inc=1, device_id={"inner": peer}, device_id_type=MESH)
    loads = [
        pltpu.make_async_copy(transfers_hbm, transfers, load_sem.at[0]),
        pltpu.make_async_copy(near_hbm, near, load_sem.at[1]),
    ]
    base_loads = [
        pltpu.make_async_copy(
            bases_hbm.at[pl.ds(k * chunk, chunk)], bases.at[pl.ds(k * chunk, chunk)], load_sem.at[2 + k]
        )
        for k in range(leaves // chunk)
    ]
    for copy in loads + base_loads:
        copy.start()
    loads[0].wait()
    leaf_fields[...] = dot(field[...], transfers[...], 1, 1).astype(BF)
    pl.semaphore_wait(barrier, 2)
    copies = []
    for k, peer in enumerate((left, right)):
        copy = pltpu.make_async_remote_copy(
            src_ref=halo.at[k], dst_ref=arrived.at[1 - k], send_sem=send_sem.at[k],
            recv_sem=recv_sem.at[1 - k], device_id={"inner": peer}, device_id_type=MESH,
        )
        copy.start()
        copies.append(copy)
    loads[1].wait()
    for k, copy in enumerate(base_loads):
        copy.wait()
        for index in range(k * chunk, (k + 1) * chunk):
            span = slice(index * leaf, (index + 1) * leaf)
            part = leaf_fields[:, index * rank : (index + 1) * rank]
            out[:, span] = near[:, span] + dot(part, bases[index], 1, 1)
    for copy in copies:
        copy.wait()
    out[:, :rim] += arrived[0]
    out[:, count - rim :] += arrived[1]


def on_device(
    points, charges, bases, transfers, parents, couplings, group_couplings, near_pairs, pair_count, far_list
):
    leaves = transfers.shape[1]
    count = points.shape[1]
    leaf = count // leaves
    dim, rhs, rank = points.shape[2], charges.shape[2], bases.shape[2]
    rim = REACH * leaf
    wide = count + 2 * rim
    inner, outer = lax.axis_size("inner"), lax.axis_size("outer")
    pt = jnp.swapaxes(points[0], 0, 1)
    ct = jnp.swapaxes(charges[0], 0, 1)
    pairs = jnp.swapaxes(near_pairs[0], 0, 1)
    leaf_bases = bases[0].reshape(leaves, leaf, rank)
    flat_transfers = transfers[0].reshape(leaves * rank, rank)
    dma = pltpu.SemaphoreType.DMA
    halo_points, halo_charges, near, field = pl.pallas_call(
        functools.partial(exchange_kernel, inner, outer, leaves),
        out_shape=[
            jax.ShapeDtypeStruct((2, dim, rim), BF),
            jax.ShapeDtypeStruct((2, rhs, rim), BF),
            jax.ShapeDtypeStruct((rhs, count), F32),
            jax.ShapeDtypeStruct((rhs, rank), BF),
        ],
        in_specs=[ANY] * 4 + [VMEM] * 3 + [SMEM],
        out_specs=[ANY, ANY, VMEM, VMEM],
        scratch_shapes=[
            pltpu.VMEM((dim, count), BF),
            pltpu.VMEM((rhs, count), BF),
            pltpu.VMEM((leaves, leaf, rank), BF),
            pltpu.VMEM((leaves * rank, rank), BF),
            pltpu.VMEM((rhs, leaves * rank), BF),
            pltpu.VMEM((2 * rhs, rank), F32),
            pltpu.VMEM((inner, 2 * rhs, rank), F32),
            pltpu.VMEM((outer, rhs, rank), BF),
            dma((3 + leaves // 8,)),
            dma((4,)),
            dma((4,)),
            dma((inner,)),
            dma((inner,)),
            dma((outer,)),
            dma((outer,)),
        ],
        compiler_params=pltpu.CompilerParams(
            vmem_limit_bytes=LIMIT, collective_id=0, has_side_effects=True
        ),
        name="exchange",
    )(pt, ct, leaf_bases, flat_transfers, parents[0, 0], couplings[0], group_couplings[0], far_list)
    near, halo = pl.pallas_call(
        functools.partial(pair_kernel, leaves, leaf),
        out_shape=[
            jax.ShapeDtypeStruct((rhs, count), F32),
            jax.ShapeDtypeStruct((2, rhs, rim), F32),
        ],
        in_specs=[SMEM, SMEM] + [ANY] * 5,
        out_specs=[ANY] * 2,
        scratch_shapes=[
            pltpu.VMEM((dim, wide), BF),
            pltpu.VMEM((rhs, wide), BF),
            pltpu.VMEM((EXTRA, wide), BF),
            pltpu.VMEM((EXTRA, wide), BF),
            pltpu.VMEM((rhs, wide), F32),
            dma((7,)),
        ],
        compiler_params=pltpu.CompilerParams(vmem_limit_bytes=LIMIT),
        name="pairs",
    )(pairs, pair_count, pt, ct, halo_points, halo_charges, near)
    out = pl.pallas_call(
        functools.partial(finish_kernel, inner),
        out_shape=jax.ShapeDtypeStruct((rhs, count), F32),
        in_specs=[ANY] * 4 + [VMEM],
        out_specs=VMEM,
        scratch_shapes=[
            pltpu.VMEM((rhs, count), F32),
            pltpu.VMEM((leaves, leaf, rank), BF),
            pltpu.VMEM((leaves * rank, rank), BF),
            pltpu.VMEM((rhs, leaves * rank), BF),
            pltpu.VMEM((2, rhs, rim), F32),
            dma((2 + leaves // 8,)),
            dma((2,)),
            dma((2,)),
        ],
        compiler_params=pltpu.CompilerParams(
            vmem_limit_bytes=LIMIT, collective_id=1, has_side_effects=True
        ),
        name="finish",
    )(halo, near, leaf_bases, flat_transfers, field)
    return jnp.swapaxes(out, 0, 1)[None]


def solution(mesh):
    placed = (
        P("outer", "inner", None),
        P("outer", "inner", None),
        P("outer", "inner", None),
        P("outer", "inner", None, None),
        P("outer", "inner", None, None),
        P("outer", "inner", None, None),
        P("outer", None, None, None),
        P("outer", "inner", None),
        P("outer", "inner"),
        P("outer", "inner"),
    )
    return jax.shard_map(
        on_device, mesh=mesh, in_specs=placed, out_specs=P("outer", "inner", None), check_vma=False
    )
```

time: 509 us -> 82.1 us (0.16)
  the two profiles are of different devices: /device:TPU:16 before, /device:TPU:120 now
where the time goes in v2:
time: 82.1 us; the launch traced here: 81.9 us
  Pallas kernels  79 us (96%)
  local copies, waits for them, and re-layouts  2.26 us (3%)
    pallas_call x1, Pallas kernels, on_device(): pl.pallas_call(functools.partial(pair_kernel, leaves, leaf), out_shape=[j...  48.7 us
    pallas_call x1, Pallas kernels, on_device(): pl.pallas_call(functools.partial(exchange_kernel, inner, outer, leaves),...  21.7 us
    pallas_call x1, Pallas kernels, on_device(): pl.pallas_call(functools.partial(finish_kernel, inner), out_shape=jax.Sha...  8.55 us
    unnamed x1, local copies, waits for them, and re-layouts  2.26 us

profile of v2, /device:TPU:120, one launch (start us, length us, event | category | flops | bytes accessed | tf_op | source)
XLA Modules:
  0.0 81.9 jit_solution(9160033027821846502)
XLA Ops:
  0.7 21.7 %exchange.1 = (bf16[2,64,2048]{2,1,0:T(8,128)(2,1)}, bf16[2,16,2048]{2,1,0:T(8,128)(2,1)}, f32[16,16384]{1,0:T(8,128)}, bf16[16,128]{1,0:T(8,128)(2,1)}) custom-call(bf16[64,16384]{1,0:T(8,128)(2,1)} %bitcast.19, bf16[16,16384]{1,0:T(8,128)(2,1)} %bitcast.24, bf16[32,512,128]{2,1,0:T(8,128)(2,1)} %bitcast.17, bf16[4096,128]{1,0:T(8,128)(2,1)} %bitcast.22, ...), custom_call_target="tpu_custom_call" | custom-call | tf_op jit(solution)/shard_map/exchange/pallas_call | solution.py:310
  22.4 48.7 %pairs.1 = (f32[16,16384]{1,0:T(8,128)}, f32[2,16,2048]{2,1,0:T(8,128)}) custom-call(s32[2,96]{1,0:T(2,128)} %bitcast.29, s32[1,1]{1,0:T(1,128)S(6)} %copy.12.live, bf16[64,16384]{1,0:T(8,128)(2,1)} %bitcast.20, bf16[16,16384]{1,0:T(8,128)(2,1)} %bitcast.25, bf16[2,64,2048]{2,1,0:T(8,128)(2,1)} %get-tuple-element.11.halo_points, ...), custom_call_target="tpu_custom_call" | custom-call | tf_op jit(solution)/shard_map/pairs/pallas_call | solution.py:342
  71.1 8.5 %finish.1 = f32[16,16384]{1,0:T(8,128)} custom-call(f32[2,16,2048]{2,1,0:T(8,128)} %get-tuple-element.14.halo, f32[16,16384]{1,0:T(8,128)} %get-tuple-element.15.near_hbm, bf16[32,512,128]{2,1,0:T(8,128)(2,1)} %bitcast.18, bf16[4096,128]{1,0:T(8,128)(2,1)} %bitcast.23, bf16[16,128]{1,0:T(8,128)(2,1)} %get-tuple-element.16.field), custom_call_target="tpu_custom_call" | custom-call | tf_op jit(solution)/shard_map/finish/pallas_call | solution.py:361
  79.7 2.3 %copy.13 = f32[1,16384,16]{1,2,0:T(8,128)} copy(f32[1,16384,16]{1,2,0:T(8,128)} %bitcast.21) | data formatting | bytes 2097152

commit v3 on v2

--- a/solution.py
+++ b/solution.py
@@ -56,7 +56,7 @@
     inner, outer, leaves,
     pt_hbm, ct_hbm, bases_hbm, transfers_hbm, parent, couplings, group_couplings, far,
     halo_points, halo_charges, near, field_out,
-    points, charges, bases, transfers, skeletons, packed, slots, group_slots,
+    points, charges, bases, transfers, skeletons, packed, slots, group_slots, tiles,
     load_sem, halo_send, halo_recv, node_send, node_recv, group_send, group_recv,
 ):
     me, group = lax.axis_index("inner"), lax.axis_index("outer")
@@ -130,18 +130,26 @@
         halo_copies.append(copy)
     loads[2].wait()
 
+    def own_tile(index, slot):
+        cols = columns(index, leaf)
+        block = points[:, cols]
+        first, second = norm_rows(block)
+        left_form = jnp.concatenate([block, first], 0)
+        right_form = jnp.concatenate([block, second], 0)
+        tiles[slot] = jnp.exp(dot(left_form, right_form, 0, 0)).astype(BF)
+
     def diagonal(index, carry):
-        cols = columns(index, leaf)
-        first, second = norm_rows(points[:, cols])
-        left_form = jnp.concatenate([points[:, cols], first], 0)
-        right_form = jnp.concatenate([points[:, cols], second], 0)
-        tile = jnp.exp(dot(left_form, right_form, 0, 0)).astype(BF)
-        own = charges[:, cols]
-        near[:, cols] = RIDGE * own.astype(F32) + dot(own, tile, 1, 0)
+        for k in range(GROUP):
+            at = index * GROUP + k
+            own_tile(jnp.minimum(at + 1, leaves - 1), (k + 1) % 2)
+            cols = columns(at, leaf)
+            own = charges[:, cols]
+            near[:, cols] = RIDGE * own.astype(F32) + dot(own, tiles[k % 2], 1, 0)
         return carry
 
-    half = leaves // 2
-    lax.fori_loop(0, half, diagonal, 0, unroll=4)
+    own_tile(0, 0)
+    half = leaves // GROUP // 2
+    lax.fori_loop(0, half, diagonal, 0)
 
     for k in range(1, inner):
         sender = lax.rem(me + k, inner)
@@ -160,7 +168,7 @@
     field = jnp.zeros((rhs, rank), F32)
     for j in range(couplings.shape[0]):
         field += dot(slots[far[0, j], :rhs].astype(BF), couplings[j], 1, 1)
-    lax.fori_loop(half, leaves, diagonal, 0, unroll=4)
+    lax.fori_loop(half, leaves // GROUP, diagonal, 0)
     group_field = jnp.zeros((rhs, rank), F32)
     for k in range(1, outer):
         sender = lax.rem(group + k, outer)
@@ -180,7 +188,7 @@
     leaves, leaf,
     pairs, live, pt_hbm, ct_hbm, halo_points, halo_charges, near_hbm,
     out_near, out_halo,
-    points, charges, firsts, seconds, totals, sem,
+    points, charges, firsts, seconds, totals, tiles, flipped, sem,
 ):
     rim = REACH * leaf
     count = leaves * leaf
@@ -209,23 +217,35 @@
 
     lax.fori_loop(0, leaves + 2 * REACH, build, 0, unroll=2)
 
-    def body(index):
-        cols_a = columns(pairs[0, index] + REACH, leaf)
-        cols_b = columns(pairs[1, index], leaf)
+    number = live[0, 0]
+
+    def spans(index):
+        return columns(pairs[0, index] + REACH, leaf), columns(pairs[1, index], leaf)
+
+    def make(index, slot):
+        cols_a, cols_b = spans(jnp.minimum(index, number - 1))
         tile = tile_of(points, firsts, seconds, cols_a, cols_b)
-        totals[:, cols_b] += dot(charges[:, cols_a], tile, 1, 0)
-        totals[:, cols_a] += dot(charges[:, cols_b], tile, 1, 1)
+        tiles[slot] = tile
+        flipped[slot] = tile.T
+
+    def use(index, slot):
+        cols_a, cols_b = spans(index)
+        totals[:, cols_b] += dot(charges[:, cols_a], tiles[slot], 1, 0)
+        totals[:, cols_a] += dot(charges[:, cols_b], flipped[slot], 1, 0)
 
     def block(index, carry):
         for k in range(GROUP):
-            body(index * GROUP + k)
+            at = index * GROUP + k
+            make(at + 1, (k + 1) % 2)
+            use(at, k % 2)
         return carry
 
     def single(index, carry):
-        body(index)
+        make(index + 1, lax.rem(index + 1, 2))
+        use(index, lax.rem(index, 2))
         return carry
 
-    number = live[0, 0]
+    make(0, 0)
     whole = number // GROUP
     lax.fori_loop(0, whole, block, 0)
     lax.fori_loop(whole * GROUP, number, single, 0)
@@ -326,6 +346,7 @@
             pltpu.VMEM((2 * rhs, rank), F32),
             pltpu.VMEM((inner, 2 * rhs, rank), F32),
             pltpu.VMEM((outer, rhs, rank), BF),
+            pltpu.VMEM((2, leaf, leaf), BF),
             dma((3 + leaves // 8,)),
             dma((4,)),
             dma((4,)),
@@ -353,6 +374,8 @@
             pltpu.VMEM((EXTRA, wide), BF),
             pltpu.VMEM((EXTRA, wide), BF),
             pltpu.VMEM((rhs, wide), F32),
+            pltpu.VMEM((2, leaf, leaf), BF),
+            pltpu.VMEM((2, leaf, leaf), BF),
             dma((7,)),
         ],
         compiler_params=pltpu.CompilerParams(vmem_limit_bytes=LIMIT),

time: 82.1 us -> 71.2 us (0.87)
  the two profiles are of different devices: /device:TPU:120 before, /device:TPU:16 now
where the time goes in v3:
time: 71.2 us; the launch traced here: 71 us
  Pallas kernels  68.1 us (96%)
  local copies, waits for them, and re-layouts  2.26 us (3%)
    pallas_call x1, Pallas kernels, on_device(): pl.pallas_call(functools.partial(pair_kernel, leaves, leaf), out_shape=[j...  35.9 us
    pallas_call x1, Pallas kernels, on_device(): pl.pallas_call(functools.partial(exchange_kernel, inner, outer, leaves),...  22.4 us
    pallas_call x1, Pallas kernels, on_device(): pl.pallas_call(functools.partial(finish_kernel, inner), out_shape=jax.Sha...  9.76 us
    unnamed x1, local copies, waits for them, and re-layouts  2.26 us

profile of v3, /device:TPU:16, one launch (start us, length us, event | category | flops | bytes accessed | tf_op | source)
XLA Modules:
  0.0 71.0 jit_solution(12961878169157533909)
XLA Ops:
  0.7 22.4 %exchange.1 = (bf16[2,64,2048]{2,1,0:T(8,128)(2,1)}, bf16[2,16,2048]{2,1,0:T(8,128)(2,1)}, f32[16,16384]{1,0:T(8,128)}, bf16[16,128]{1,0:T(8,128)(2,1)}) custom-call(bf16[64,16384]{1,0:T(8,128)(2,1)} %bitcast.19, bf16[16,16384]{1,0:T(8,128)(2,1)} %bitcast.24, bf16[32,512,128]{2,1,0:T(8,128)(2,1)} %bitcast.17, bf16[4096,128]{1,0:T(8,128)(2,1)} %bitcast.22, ...), custom_call_target="tpu_custom_call" | custom-call | tf_op jit(solution)/shard_map/exchange/pallas_call | solution.py:330
  23.1 35.9 %pairs.1 = (f32[16,16384]{1,0:T(8,128)}, f32[2,16,2048]{2,1,0:T(8,128)}) custom-call(s32[2,96]{1,0:T(2,128)} %bitcast.29, s32[1,1]{1,0:T(1,128)S(6)} %copy.12.live, bf16[64,16384]{1,0:T(8,128)(2,1)} %bitcast.20, bf16[16,16384]{1,0:T(8,128)(2,1)} %bitcast.25, bf16[2,64,2048]{2,1,0:T(8,128)(2,1)} %get-tuple-element.11.halo_points, ...), custom_call_target="tpu_custom_call" | custom-call | tf_op jit(solution)/shard_map/pairs/pallas_call | solution.py:363
  59.0 9.8 %finish.1 = f32[16,16384]{1,0:T(8,128)} custom-call(f32[2,16,2048]{2,1,0:T(8,128)} %get-tuple-element.14.halo, f32[16,16384]{1,0:T(8,128)} %get-tuple-element.15.near_hbm, bf16[32,512,128]{2,1,0:T(8,128)(2,1)} %bitcast.18, bf16[4096,128]{1,0:T(8,128)(2,1)} %bitcast.23, bf16[16,128]{1,0:T(8,128)(2,1)} %get-tuple-element.16.field), custom_call_target="tpu_custom_call" | custom-call | tf_op jit(solution)/shard_map/finish/pallas_call | solution.py:384
  68.8 2.3 %copy.13 = f32[1,16384,16]{1,2,0:T(8,128)} copy(f32[1,16384,16]{1,2,0:T(8,128)} %bitcast.21) | data formatting | bytes 2097152

commit v4 on v3

v4 whole, which is shorter than its diff:
```python
import functools

import jax
import jax.numpy as jnp
from jax import lax
from jax.experimental import pallas as pl
from jax.experimental.pallas import tpu as pltpu
from jax.sharding import PartitionSpec as P

REACH = 4
RIDGE = 0.25
EXTRA = 16
GROUP = 4
ROOTS = 2
BF = jnp.bfloat16
F32 = jnp.float32
VMEM = pl.BlockSpec(memory_space=pltpu.VMEM)
SMEM = pl.BlockSpec(memory_space=pltpu.SMEM)
ANY = pl.BlockSpec(memory_space=pl.ANY)
MESH = pl.DeviceIdType.MESH
LIMIT = 56 * 2**20


def dot(left, right, left_dim, right_dim):
    return lax.dot_general(
        left, right, (((left_dim,), (right_dim,)), ((), ())), preferred_element_type=F32
    )


def norm_rows(block):
    wide = block.astype(F32)
    total = 0.5 * jnp.sum(wide * wide, 0, keepdims=True)
    high = total.astype(BF).astype(F32)
    rest = total - high
    middle = rest.astype(BF).astype(F32)
    parts = (high, middle, rest - middle)
    row = lax.broadcasted_iota(jnp.int32, (EXTRA, block.shape[1]), 0)
    first = jnp.where((row >= 3) & (row < 6), 1.0, 0.0)
    second = jnp.where(row < 3, 1.0, 0.0)
    for k in range(3):
        first = jnp.where(row == k, -parts[k], first)
        second = jnp.where(row == 3 + k, -parts[k], second)
    return first.astype(BF), second.astype(BF)


def columns(index, width):
    return pl.ds(pl.multiple_of(index * width, width), width)


def tile_of(points, firsts, seconds, cols_a, cols_b):
    left = jnp.concatenate([points[:, cols_a], firsts[:, cols_a]], 0)
    right = jnp.concatenate([points[:, cols_b], seconds[:, cols_b]], 0)
    return jnp.exp(dot(left, right, 0, 0)).astype(BF)


def exchange_kernel(
    inner, outer, leaves,
    pt_hbm, ct_hbm, bases_hbm, transfers_hbm, parent, couplings, group_couplings, far,
    halo_points, halo_charges, near, field_out,
    points, charges, bases, transfers, skeletons, term, slots, gathered, halves, group_field, tiles,
    load_sem, halo_send, halo_recv, node_send, node_recv, term_send, term_recv,
    half_send, half_recv, field_send, field_recv,
):
    me, group = lax.axis_index("inner"), lax.axis_index("outer")
    right, left = lax.rem(me + 1, inner), lax.rem(me + inner - 1, inner)
    rhs, count = ct_hbm.shape
    leaf = count // leaves
    rim = REACH * leaf
    rank = parent.shape[1]
    chunk = 8
    rows = rhs // ROOTS
    roots = [h * (inner // ROOTS) for h in range(ROOTS)]
    is_root = functools.reduce(jnp.logical_or, [me == root for root in roots])
    peers = [lax.rem(me + k, inner) for k in range(1, inner)]
    others = [lax.rem(group + k, outer) for k in range(1, outer)]
    loads = [
        pltpu.make_async_copy(ct_hbm, charges, load_sem.at[0]),
        pltpu.make_async_copy(transfers_hbm, transfers, load_sem.at[1]),
        pltpu.make_async_copy(pt_hbm, points, load_sem.at[2]),
    ]
    base_loads = [
        pltpu.make_async_copy(
            bases_hbm.at[pl.ds(k * chunk, chunk)], bases.at[pl.ds(k * chunk, chunk)], load_sem.at[3 + k]
        )
        for k in range(leaves // chunk)
    ]
    loads[0].start()
    for copy in base_loads:
        copy.start()
    loads[1].start()
    loads[2].start()
    barrier = pltpu.get_barrier_semaphore()
    for peer in peers:
        pl.semaphore_signal(barrier, inc=1, device_id={"inner": peer}, device_id_type=MESH)

    @pl.when(is_root)
    def _():
        for other in others:
            pl.semaphore_signal(barrier, inc=1, device_id={"outer": other}, device_id_type=MESH)

    loads[0].wait()
    for k, copy in enumerate(base_loads):
        copy.wait()
        for index in range(k * chunk, (k + 1) * chunk):
            block = charges[:, index * leaf : (index + 1) * leaf]
            skeletons[:, index * rank : (index + 1) * rank] = dot(block, bases[index], 1, 0).astype(BF)
    loads[1].wait()
    node = dot(skeletons[...], transfers[...], 1, 0).astype(BF)
    slots[me] = node
    term[...] = dot(node, parent[...], 1, 0)
    gathered[me] = term[:rows]
    for h in range(1, ROOTS):

        @pl.when(me == roots[h])
        def _(h=h):
            gathered[me] = term[h * rows : (h + 1) * rows]

    @pl.when(is_root)
    def _():
        pl.semaphore_wait(barrier, inner + outer - 2)

    @pl.when(jnp.logical_not(is_root))
    def _():
        pl.semaphore_wait(barrier, inner - 1)

    def remote(source, target, send, recv, **where):
        return pltpu.make_async_remote_copy(
            src_ref=source, dst_ref=target, send_sem=send, recv_sem=recv,
            device_id=where, device_id_type=MESH,
        )

    term_copies = [
        remote(term.at[pl.ds(h * rows, rows)], gathered.at[me], term_send.at[h], term_recv.at[me], inner=root)
        for h, root in enumerate(roots)
    ]
    for root, copy in zip(roots, term_copies):
        pl.when(me != root)(copy.start)
    halo_copies = [
        remote(
            source.at[:, pl.ds(begin, rim)], target, halo_send.at[k], halo_recv.at[k], inner=peer
        )
        for k, (source, target, peer, begin) in enumerate((
            (pt_hbm, halo_points.at[0], right, count - rim),
            (pt_hbm, halo_points.at[1], left, 0),
            (ct_hbm, halo_charges.at[0], right, count - rim),
            (ct_hbm, halo_charges.at[1], left, 0),
        ))
    ]
    node_copies = [
        remote(slots.at[me], slots.at[me], node_send.at[k], node_recv.at[me], inner=peer)
        for k, peer in enumerate(peers)
    ]
    half_copies = [
        remote(halves.at[group], halves.at[group], half_send.at[k], half_recv.at[group], outer=other)
        for k, other in enumerate(others)
    ]
    field_copies = [
        [
            remote(group_field.at[h], group_field.at[h], field_send.at[k], field_recv.at[h], inner=peer)
            for k, peer in enumerate(peers)
        ]
        for h in range(ROOTS)
    ]
    for copy in halo_copies + node_copies:
        copy.start()
    loads[2].wait()
    edge = leaf // 2

    def own_tile(index, slot):
        block = points[:, columns(index, leaf)]
        first, second = norm_rows(block)
        left_form = jnp.concatenate([block, first], 0)
        right_form = jnp.concatenate([block, second], 0)
        upper = jnp.exp(dot(left_form[:, :edge], right_form, 0, 0)).astype(BF)
        tiles[slot, :edge] = upper
        tiles[slot, edge:, :edge] = upper[:, edge:].T
        tiles[slot, edge:, edge:] = jnp.exp(
            dot(left_form[:, edge:], right_form[:, edge:], 0, 0)
        ).astype(BF)

    def diagonal(index, carry):
        for k in range(GROUP):
            at = index * GROUP + k
            own_tile(jnp.minimum(at + 1, leaves - 1), (k + 1) % 2)
            cols = columns(at, leaf)
            own = charges[:, cols]
            near[:, cols] = RIDGE * own.astype(F32) + dot(own, tiles[k % 2], 1, 0)
        return carry

    own_tile(0, 0)
    total = leaves // GROUP
    stops = (3 * total // 8, 5 * total // 8)
    lax.fori_loop(0, stops[0], diagonal, 0)

    @pl.when(is_root)
    def _():
        for peer in peers:
            pltpu.make_async_copy(gathered.at[me], gathered.at[peer], term_recv.at[peer]).wait()
        halves[group] = jnp.sum(gathered[...], 0).astype(BF).astype(F32)
        for copy in half_copies:
            copy.start()

    lax.fori_loop(stops[0], stops[1], diagonal, 0)
    for h, root in enumerate(roots):

        @pl.when(me == root)
        def _(h=h):
            part = jnp.zeros((rows, rank), F32)
            for other in others:
                pltpu.make_async_copy(halves.at[group], halves.at[other], half_recv.at[other]).wait()
                part += dot(halves[other].astype(BF), group_couplings[other], 1, 1)
            group_field[h] = part.astype(BF).astype(F32)
            for copy in field_copies[h]:
                copy.start()

    lax.fori_loop(stops[1], total, diagonal, 0)
    for peer in peers:
        pltpu.make_async_copy(slots.at[me], slots.at[peer], node_recv.at[peer]).wait()
    field = jnp.zeros((rhs, rank), F32)
    for j in range(couplings.shape[0]):
        field += dot(slots[far[0, j]], couplings[j], 1, 1)
    for h, root in enumerate(roots):

        @pl.when(me != root)
        def _(h=h):
            pltpu.make_async_copy(group_field.at[h], group_field.at[h], field_recv.at[h]).wait()

    whole = jnp.concatenate([group_field[h] for h in range(ROOTS)], 0).astype(BF)
    field_out[...] = (field + dot(whole, parent[...], 1, 1)).astype(BF)
    for root, copy in zip(roots, term_copies):
        pl.when(me != root)(copy.wait_send)
    for copy in node_copies:
        copy.wait_send()
    for h, root in enumerate(roots):

        @pl.when(me == root)
        def _(h=h):
            for copy in half_copies + field_copies[h]:
                copy.wait_send()

    for copy in halo_copies:
        copy.wait()


def pair_kernel(
    leaves, leaf,
    pairs, live, pt_hbm, ct_hbm, halo_points, halo_charges,
    out_near, out_halo,
    points, charges, firsts, seconds, totals, tiles, flipped, sem,
):
    rim = REACH * leaf
    count = leaves * leaf
    chunk = 8
    spots = (pl.ds(0, rim), pl.ds(rim + count, rim))
    own = pl.ds(rim, count)
    copies = [
        pltpu.make_async_copy(halo_points.at[0], points.at[:, spots[0]], sem.at[0]),
        pltpu.make_async_copy(halo_points.at[1], points.at[:, spots[1]], sem.at[1]),
    ]
    copies += [
        pltpu.make_async_copy(
            pt_hbm.at[:, pl.ds(k * chunk * leaf, chunk * leaf)],
            points.at[:, pl.ds(rim + k * chunk * leaf, chunk * leaf)],
            sem.at[2 + k],
        )
        for k in range(leaves // chunk)
    ]
    at = len(copies)
    charge_copies = [
        pltpu.make_async_copy(ct_hbm, charges.at[:, own], sem.at[at]),
        pltpu.make_async_copy(halo_charges.at[0], charges.at[:, spots[0]], sem.at[at + 1]),
        pltpu.make_async_copy(halo_charges.at[1], charges.at[:, spots[1]], sem.at[at + 2]),
    ]
    for copy in copies + charge_copies:
        copy.start()
    totals[...] = jnp.zeros_like(totals)

    def build(index, carry):
        cols = columns(index, leaf)
        firsts[:, cols], seconds[:, cols] = norm_rows(points[:, cols])
        return carry

    spans_built = [(0, REACH), (REACH + leaves, 2 * REACH + leaves)]
    spans_built += [(REACH + k * chunk, REACH + (k + 1) * chunk) for k in range(leaves // chunk)]
    for copy, (low, high) in zip(copies, spans_built):
        copy.wait()
        lax.fori_loop(low, high, build, 0, unroll=2)
    for copy in charge_copies:
        copy.wait()
    number = live[0, 0]

    def spans(index):
        return columns(pairs[0, index] + REACH, leaf), columns(pairs[1, index], leaf)

    def make(index, slot):
        cols_a, cols_b = spans(jnp.minimum(index, number - 1))
        tile = tile_of(points, firsts, seconds, cols_a, cols_b)
        tiles[slot] = tile
        flipped[slot] = tile.T

    def use(index, slot):
        cols_a, cols_b = spans(index)
        totals[:, cols_b] += dot(charges[:, cols_a], tiles[slot], 1, 0)
        totals[:, cols_a] += dot(charges[:, cols_b], flipped[slot], 1, 0)

    def block(index, carry):
        for k in range(GROUP):
            at = index * GROUP + k
            make(at + 1, (k + 1) % 2)
            use(at, k % 2)
        return carry

    def single(index, carry):
        make(index + 1, lax.rem(index + 1, 2))
        use(index, lax.rem(index, 2))
        return carry

    make(0, 0)
    whole = number // GROUP
    lax.fori_loop(0, whole, block, 0)
    lax.fori_loop(whole * GROUP, number, single, 0)
    write = pltpu.make_async_copy(totals.at[:, own], out_near, sem.at[0])
    write.start()
    for k, spot in enumerate(spots):
        out_halo[k] = totals[:, spot].astype(BF)
    write.wait()


def finish_kernel(
    inner,
    halo, near_hbm, own_hbm, bases_hbm, transfers_hbm, field,
    out, arrived,
    near, own, bases, transfers, leaf_fields, load_sem, store_sem, send_sem, recv_sem,
):
    me = lax.axis_index("inner")
    right, left = lax.rem(me + 1, inner), lax.rem(me + inner - 1, inner)
    leaves, leaf, rank = bases.shape
    chunk = 8
    parts = leaves // chunk
    width = chunk * leaf
    barrier = pltpu.get_barrier_semaphore()
    for peer in (left, right):
        pl.semaphore_signal(barrier, inc=1, device_id={"inner": peer}, device_id_type=MESH)
    loads = [pltpu.make_async_copy(transfers_hbm, transfers, load_sem.at[0])]
    near_loads, own_loads, base_loads = [], [], []
    for k in range(parts):
        span = pl.ds(k * width, width)
        leaf_span = pl.ds(k * chunk, chunk)
        base_loads.append(
            pltpu.make_async_copy(bases_hbm.at[leaf_span], bases.at[leaf_span], load_sem.at[1 + k])
        )
        near_loads.append(
            pltpu.make_async_copy(near_hbm.at[:, span], near.at[:, span], load_sem.at[1 + parts + k])
        )
        own_loads.append(
            pltpu.make_async_copy(own_hbm.at[:, span], own.at[:, span], load_sem.at[1 + 2 * parts + k])
        )
    loads[0].start()
    for group in zip(base_loads, near_loads, own_loads):
        for copy in group:
            copy.start()
    pl.semaphore_wait(barrier, 2)
    copies = []
    for k, peer in enumerate((left, right)):
        copy = pltpu.make_async_remote_copy(
            src_ref=halo.at[k], dst_ref=arrived.at[1 - k], send_sem=send_sem.at[k],
            recv_sem=recv_sem.at[1 - k], device_id={"inner": peer}, device_id_type=MESH,
        )
        copy.start()
        copies.append(copy)
    loads[0].wait()
    leaf_fields[...] = dot(field[...], transfers[...], 1, 1).astype(BF)
    stores = []
    for k in range(parts):
        base_loads[k].wait()
        near_loads[k].wait()
        own_loads[k].wait()
        for index in range(k * chunk, (k + 1) * chunk):
            span = slice(index * leaf, (index + 1) * leaf)
            part = leaf_fields[:, index * rank : (index + 1) * rank]
            near[:, span] += own[:, span] + dot(part, bases[index], 1, 1)
        span = pl.ds(k * width, width)
        store = pltpu.make_async_copy(near.at[:, span], out.at[:, span], store_sem.at[k])
        store.start()
        stores.append(store)
    for copy in stores + copies:
        copy.wait()


def on_device(
    points, charges, bases, transfers, parents, couplings, group_couplings, near_pairs, pair_count, far_list
):
    leaves = transfers.shape[1]
    count = points.shape[1]
    leaf = count // leaves
    dim, rhs, rank = points.shape[2], charges.shape[2], bases.shape[2]
    rim = REACH * leaf
    wide = count + 2 * rim
    inner, outer = lax.axis_size("inner"), lax.axis_size("outer")
    pt = jnp.swapaxes(points[0], 0, 1)
    ct = jnp.swapaxes(charges[0], 0, 1)
    pairs = jnp.swapaxes(near_pairs[0], 0, 1)
    leaf_bases = bases[0].reshape(leaves, leaf, rank)
    flat_transfers = transfers[0].reshape(leaves * rank, rank)
    dma = pltpu.SemaphoreType.DMA
    parts = leaves // 8
    halo_points, halo_charges, own, field = pl.pallas_call(
        functools.partial(exchange_kernel, inner, outer, leaves),
        out_shape=[
            jax.ShapeDtypeStruct((2, dim, rim), BF),
            jax.ShapeDtypeStruct((2, rhs, rim), BF),
            jax.ShapeDtypeStruct((rhs, count), F32),
            jax.ShapeDtypeStruct((rhs, rank), BF),
        ],
        in_specs=[ANY] * 4 + [VMEM] * 3 + [SMEM],
        out_specs=[ANY, ANY, VMEM, VMEM],
        scratch_shapes=[
            pltpu.VMEM((dim, count), BF),
            pltpu.VMEM((rhs, count), BF),
            pltpu.VMEM((leaves, leaf, rank), BF),
            pltpu.VMEM((leaves * rank, rank), BF),
            pltpu.VMEM((rhs, leaves * rank), BF),
            pltpu.VMEM((rhs, rank), F32),
            pltpu.VMEM((inner, rhs, rank), BF),
            pltpu.VMEM((inner, rhs // ROOTS, rank), F32),
            pltpu.VMEM((outer, rhs // ROOTS, rank), F32),
            pltpu.VMEM((ROOTS, rhs // ROOTS, rank), F32),
            pltpu.VMEM((2, leaf, leaf), BF),
            dma((3 + parts,)),
            dma((4,)),
            dma((4,)),
            dma((inner,)),
            dma((inner,)),
            dma((ROOTS,)),
            dma((inner,)),
            dma((outer,)),
            dma((outer,)),
            dma((inner,)),
            dma((ROOTS,)),
        ],
        compiler_params=pltpu.CompilerParams(
            vmem_limit_bytes=LIMIT, collective_id=0, has_side_effects=True
        ),
        name="exchange",
    )(pt, ct, leaf_bases, flat_transfers, parents[0, 0], couplings[0], group_couplings[0], far_list)
    near, halo = pl.pallas_call(
        functools.partial(pair_kernel, leaves, leaf),
        out_shape=[
            jax.ShapeDtypeStruct((rhs, count), F32),
            jax.ShapeDtypeStruct((2, rhs, rim), BF),
        ],
        in_specs=[SMEM, SMEM] + [ANY] * 4,
        out_specs=[ANY, VMEM],
        scratch_shapes=[
            pltpu.VMEM((dim, wide), BF),
            pltpu.VMEM((rhs, wide), BF),
            pltpu.VMEM((EXTRA, wide), BF),
            pltpu.VMEM((EXTRA, wide), BF),
            pltpu.VMEM((rhs, wide), F32),
            pltpu.VMEM((2, leaf, leaf), BF),
            pltpu.VMEM((2, leaf, leaf), BF),
            dma((5 + parts,)),
        ],
        compiler_params=pltpu.CompilerParams(vmem_limit_bytes=LIMIT),
        name="pairs",
    )(pairs, pair_count, pt, ct, halo_points, halo_charges)
    main, arrived = pl.pallas_call(
        functools.partial(finish_kernel, inner),
        out_shape=[
            jax.ShapeDtypeStruct((rhs, count), F32),
            jax.ShapeDtypeStruct((2, rhs, rim), BF),
        ],
        in_specs=[ANY] * 5 + [VMEM],
        out_specs=[ANY, ANY],
        scratch_shapes=[
            pltpu.VMEM((rhs, count), F32),
            pltpu.VMEM((rhs, count), F32),
            pltpu.VMEM((leaves, leaf, rank), BF),
            pltpu.VMEM((leaves * rank, rank), BF),
            pltpu.VMEM((rhs, leaves * rank), BF),
            dma((1 + 3 * parts,)),
            dma((parts,)),
            dma((2,)),
            dma((2,)),
        ],
        compiler_params=pltpu.CompilerParams(
            vmem_limit_bytes=LIMIT, collective_id=1, has_side_effects=True
        ),
        name="finish",
    )(halo, near, own, leaf_bases, flat_transfers, field)
    middle = jnp.zeros((rhs, count - 2 * rim), F32)
    out = main + jnp.concatenate([arrived[0].astype(F32), middle, arrived[1].astype(F32)], 1)
    return jnp.swapaxes(out, 0, 1)[None]


def solution(mesh):
    placed = (
        P("outer", "inner", None),
        P("outer", "inner", None),
        P("outer", "inner", None),
        P("outer", "inner", None, None),
        P("outer", "inner", None, None),
        P("outer", "inner", None, None),
        P("outer", None, None, None),
        P("outer", "inner", None),
        P("outer", "inner"),
        P("outer", "inner"),
    )
    return jax.shard_map(
        on_device, mesh=mesh, in_specs=placed, out_specs=P("outer", "inner", None), check_vma=False
    )
```

time: 71.2 us -> 70.1 us (0.985)
  other arithmetic: 0 us -> 3.22 us
  local copies, waits for them, and re-layouts: 2.26 us -> 0.01 us
  Pallas kernels: 68.1 us -> 65.9 us
    broadcast_in_dim x0 -> x1, other arithmetic: none -> 2.32 us  [on_device(): return jnp.swapaxes(out, 0, 1)[None]]
    unnamed x1 -> x0, local copies, waits for them, and re-layouts: 2.26 us -> none
    pallas_call x1, Pallas kernels: 9.76 us -> 8.26 us  [on_device(): pl.pallas_call(functools.partial(finish_kernel, inner), out_shape=[jax.Sh...]
    pallas_call x1, Pallas kernels: 22.4 us -> 21.4 us  [on_device(): pl.pallas_call(functools.partial(exchange_kernel, inner, outer, leaves),...]
    convert_element_type x0 -> x1, other arithmetic: none -> 0.89 us  [on_device(): arrived[0].astype(F32)]
where the time goes in v4:
time: 70.1 us; the launch traced here: 69.9 us
  Pallas kernels  65.9 us (94%)
  other arithmetic  3.22 us (5%)
    pallas_call x1, Pallas kernels, on_device(): pl.pallas_call(functools.partial(pair_kernel, leaves, leaf), out_shape=[j...  36.2 us
    pallas_call x1, Pallas kernels, on_device(): pl.pallas_call(functools.partial(exchange_kernel, inner, outer, leaves),...  21.4 us
    pallas_call x1, Pallas kernels, on_device(): pl.pallas_call(functools.partial(finish_kernel, inner), out_shape=[jax.Sh...  8.26 us
    broadcast_in_dim x1, other arithmetic, on_device(): return jnp.swapaxes(out, 0, 1)[None]  2.32 us

profile of v4, /device:TPU:16, one launch (start us, length us, event | category | flops | bytes accessed | tf_op | source)
XLA Modules:
  0.0 69.9 jit_solution(6975339260649053742)
XLA Ops:
  0.0 21.4 %exchange.1 = (bf16[2,64,2048]{2,1,0:T(8,128)(2,1)}, bf16[2,16,2048]{2,1,0:T(8,128)(2,1)}, f32[16,16384]{1,0:T(8,128)}, bf16[16,128]{1,0:T(8,128)(2,1)}) custom-call(bf16[64,16384]{1,0:T(8,128)(2,1)} %bitcast.26, bf16[16,16384]{1,0:T(8,128)(2,1)} %bitcast.30, bf16[32,512,128]{2,1,0:T(8,128)(2,1)} %bitcast.24, bf16[4096,128]{1,0:T(8,128)(2,1)} %bitcast.28, ...), custom_call_target="tpu_custom_call" | custom-call | tf_op jit(solution)/shard_map/exchange/pallas_call | solution.py:407
  22.1 36.2 %pairs.1 = (f32[16,16384]{1,0:T(8,128)}, bf16[2,16,2048]{2,1,0:T(8,128)(2,1)}) custom-call(s32[2,96]{1,0:T(2,128)} %bitcast.35, s32[1,1]{1,0:T(1,128)S(6)} %copy.11.live, bf16[64,16384]{1,0:T(8,128)(2,1)} %bitcast.27, bf16[16,16384]{1,0:T(8,128)(2,1)} %bitcast.31, bf16[2,64,2048]{2,1,0:T(8,128)(2,1)} %get-tuple-element.13.halo_points, ...), custom_call_target="tpu_custom_call" | custom-call | tf_op jit(solution)/shard_map/pairs/pallas_call | solution.py:446
  58.3 8.3 %finish.1 = (f32[16,16384]{1,0:T(8,128)}, bf16[2,16,2048]{2,1,0:T(8,128)(2,1)}) custom-call(bf16[2,16,2048]{2,1,0:T(8,128)(2,1)} %get-tuple-element.15.halo, f32[16,16384]{1,0:T(8,128)} %get-tuple-element.16.near_hbm, f32[16,16384]{1,0:T(8,128)} %get-tuple-element.17.own_hbm, bf16[32,512,128]{2,1,0:T(8,128)(2,1)} %bitcast.25, bf16[4096,128]{1,0:T(8,128)(2,1)} %bitcast.29, ...), custom_call_target="tpu_custom_call" | custom-call | tf_op jit(solution)/shard_map/finish/pallas_call | solution.py:467
  66.6 0.9 %bitcast_convert_fusion.1 = (f32[16,2048]{1,0:T(8,128)S(1)}, f32[16,2048]{1,0:T(8,128)S(1)}) fusion(bf16[2,16,2048]{2,1,0:T(8,128)(2,1)} %get-tuple-element.20), kind=kLoop, calls=%fused_computation.3 | loop fusion | flops 65536 | bytes 393216 | tf_op jit(solution)/shard_map/convert_element_type | solution.py:492
  67.5 2.3 %fusion = f32[1,16384,16]{1,2,0:T(8,128)} fusion(f32[16,16384]{1,0:T(8,128)} %get-tuple-element.19, f32[16,2048]{1,0:T(8,128)S(1)} %get-tuple-element.22, f32[16,2048]{1,0:T(8,128)S(1)} %get-tuple-element.21, f32[16384]{0:T(1024)S(1)} %pad.1.clone), kind=kLoop, calls=%fused_computation.1 | loop fusion | flops 786432 | bytes 2424832 | tf_op jit(solution)/shard_map/broadcast_in_dim | solution.py:493
  (2 shorter events, 0.0 us)

commit v5 on v4

--- a/solution.py
+++ b/solution.py
@@ -55,11 +55,12 @@
 
 def exchange_kernel(
     inner, outer, leaves,
-    pt_hbm, ct_hbm, bases_hbm, transfers_hbm, parent, couplings, group_couplings, far,
-    halo_points, halo_charges, near, field_out,
-    points, charges, bases, transfers, skeletons, term, slots, gathered, halves, group_field, tiles,
-    load_sem, halo_send, halo_recv, node_send, node_recv, term_send, term_recv,
-    half_send, half_recv, field_send, field_recv,
+    pt_hbm, ct_hbm, bases_hbm, transfers_hbm, parent_hbm, couplings_hbm, group_couplings_hbm, far,
+    halo_points, halo_charges, near_hbm, field_out,
+    points, charges, bases, transfers, parent, couplings, group_couplings, near,
+    skeletons, term, slots, gathered, group_field, tiles,
+    load_sem, near_sem, halo_send, halo_recv, node_send, node_recv, term_send, term_recv,
+    field_send, field_recv,
 ):
     me, group = lax.axis_index("inner"), lax.axis_index("outer")
     right, left = lax.rem(me + 1, inner), lax.rem(me + inner - 1, inner)
@@ -77,26 +78,35 @@
         pltpu.make_async_copy(ct_hbm, charges, load_sem.at[0]),
         pltpu.make_async_copy(transfers_hbm, transfers, load_sem.at[1]),
         pltpu.make_async_copy(pt_hbm, points, load_sem.at[2]),
+        pltpu.make_async_copy(parent_hbm, parent, load_sem.at[3]),
+        pltpu.make_async_copy(couplings_hbm, couplings, load_sem.at[4]),
+        pltpu.make_async_copy(group_couplings_hbm, group_couplings, load_sem.at[5]),
     ]
     base_loads = [
         pltpu.make_async_copy(
-            bases_hbm.at[pl.ds(k * chunk, chunk)], bases.at[pl.ds(k * chunk, chunk)], load_sem.at[3 + k]
+            bases_hbm.at[pl.ds(k * chunk, chunk)], bases.at[pl.ds(k * chunk, chunk)], load_sem.at[6 + k]
         )
         for k in range(leaves // chunk)
     ]
     loads[0].start()
     for copy in base_loads:
         copy.start()
-    loads[1].start()
-    loads[2].start()
+    for k in (1, 3, 2, 4, 5):
+        loads[k].start()
     barrier = pltpu.get_barrier_semaphore()
     for peer in peers:
         pl.semaphore_signal(barrier, inc=1, device_id={"inner": peer}, device_id_type=MESH)
 
     @pl.when(is_root)
     def _():
-        for other in others:
-            pl.semaphore_signal(barrier, inc=1, device_id={"outer": other}, device_id_type=MESH)
+        def greet(index, carry):
+            for other in others:
+                pl.semaphore_signal(
+                    barrier, inc=1, device_id={"inner": index, "outer": other}, device_id_type=MESH
+                )
+            return carry
+
+        lax.fori_loop(0, inner, greet, 0)
 
     loads[0].wait()
     for k, copy in enumerate(base_loads):
@@ -107,21 +117,9 @@
     loads[1].wait()
     node = dot(skeletons[...], transfers[...], 1, 0).astype(BF)
     slots[me] = node
+    loads[3].wait()
     term[...] = dot(node, parent[...], 1, 0)
-    gathered[me] = term[:rows]
-    for h in range(1, ROOTS):
-
-        @pl.when(me == roots[h])
-        def _(h=h):
-            gathered[me] = term[h * rows : (h + 1) * rows]
-
-    @pl.when(is_root)
-    def _():
-        pl.semaphore_wait(barrier, inner + outer - 2)
-
-    @pl.when(jnp.logical_not(is_root))
-    def _():
-        pl.semaphore_wait(barrier, inner - 1)
+    pl.semaphore_wait(barrier, inner - 1 + ROOTS * (outer - 1))
 
     def remote(source, target, send, recv, **where):
         return pltpu.make_async_remote_copy(
@@ -129,12 +127,17 @@
             device_id=where, device_id_type=MESH,
         )
 
+    mine = group * inner + me
     term_copies = [
-        remote(term.at[pl.ds(h * rows, rows)], gathered.at[me], term_send.at[h], term_recv.at[me], inner=root)
+        remote(
+            term.at[pl.ds(h * rows, rows)], gathered.at[mine],
+            term_send.at[h * outer + k], term_recv.at[mine], inner=root, outer=other,
+        )
         for h, root in enumerate(roots)
-    ]
-    for root, copy in zip(roots, term_copies):
-        pl.when(me != root)(copy.start)
+        for k, other in enumerate(others)
+    ]
+    for copy in term_copies:
+        copy.start()
     halo_copies = [
         remote(
             source.at[:, pl.ds(begin, rim)], target, halo_send.at[k], halo_recv.at[k], inner=peer
@@ -149,10 +152,6 @@
     node_copies = [
         remote(slots.at[me], slots.at[me], node_send.at[k], node_recv.at[me], inner=peer)
         for k, peer in enumerate(peers)
-    ]
-    half_copies = [
-        remote(halves.at[group], halves.at[group], half_send.at[k], half_recv.at[group], outer=other)
-        for k, other in enumerate(others)
     ]
     field_copies = [
         [
@@ -189,31 +188,37 @@
 
     own_tile(0, 0)
     total = leaves // GROUP
-    stops = (3 * total // 8, 5 * total // 8)
-    lax.fori_loop(0, stops[0], diagonal, 0)
-
-    @pl.when(is_root)
-    def _():
-        for peer in peers:
-            pltpu.make_async_copy(gathered.at[me], gathered.at[peer], term_recv.at[peer]).wait()
-        halves[group] = jnp.sum(gathered[...], 0).astype(BF).astype(F32)
-        for copy in half_copies:
-            copy.start()
-
-    lax.fori_loop(stops[0], stops[1], diagonal, 0)
+    stop = 5 * total // 8
+    lax.fori_loop(0, stop, diagonal, 0)
+    spans = [pl.ds(0, stop * GROUP * leaf), pl.ds(stop * GROUP * leaf, (total - stop) * GROUP * leaf)]
+    near_copies = [
+        pltpu.make_async_copy(near.at[:, span], near_hbm.at[:, span], near_sem.at[k])
+        for k, span in enumerate(spans)
+    ]
+    near_copies[0].start()
+    loads[4].wait()
+    loads[5].wait()
     for h, root in enumerate(roots):
 
         @pl.when(me == root)
         def _(h=h):
             part = jnp.zeros((rows, rank), F32)
             for other in others:
-                pltpu.make_async_copy(halves.at[group], halves.at[other], half_recv.at[other]).wait()
-                part += dot(halves[other].astype(BF), group_couplings[other], 1, 1)
+
+                def arrive(index, carry):
+                    sender = other * inner + index
+                    pltpu.make_async_copy(gathered.at[mine], gathered.at[sender], term_recv.at[sender]).wait()
+                    return carry
+
+                lax.fori_loop(0, inner, arrive, 0)
+                skeleton = jnp.sum(gathered[pl.ds(other * inner, inner)], 0).astype(BF)
+                part += dot(skeleton, group_couplings[other], 1, 1)
             group_field[h] = part.astype(BF).astype(F32)
             for copy in field_copies[h]:
                 copy.start()
 
-    lax.fori_loop(stops[1], total, diagonal, 0)
+    lax.fori_loop(stop, total, diagonal, 0)
+    near_copies[1].start()
     for peer in peers:
         pltpu.make_async_copy(slots.at[me], slots.at[peer], node_recv.at[peer]).wait()
     field = jnp.zeros((rhs, rank), F32)
@@ -227,17 +232,17 @@
 
     whole = jnp.concatenate([group_field[h] for h in range(ROOTS)], 0).astype(BF)
     field_out[...] = (field + dot(whole, parent[...], 1, 1)).astype(BF)
-    for root, copy in zip(roots, term_copies):
-        pl.when(me != root)(copy.wait_send)
-    for copy in node_copies:
+    for copy in term_copies + node_copies:
         copy.wait_send()
     for h, root in enumerate(roots):
 
         @pl.when(me == root)
         def _(h=h):
-            for copy in half_copies + field_copies[h]:
+            for copy in field_copies[h]:
                 copy.wait_send()
 
+    for copy in near_copies:
+        copy.wait()
     for copy in halo_copies:
         copy.wait()
 
@@ -246,7 +251,7 @@
     leaves, leaf,
     pairs, live, pt_hbm, ct_hbm, halo_points, halo_charges,
     out_near, out_halo,
-    points, charges, firsts, seconds, totals, tiles, flipped, sem,
+    points, charges, firsts, seconds, totals, tiles, flipped, halo, sem,
 ):
     rim = REACH * leaf
     count = leaves * leaf
@@ -322,15 +327,18 @@
     write = pltpu.make_async_copy(totals.at[:, own], out_near, sem.at[0])
     write.start()
     for k, spot in enumerate(spots):
-        out_halo[k] = totals[:, spot].astype(BF)
+        halo[k] = totals[:, spot].astype(BF)
+    halo_write = pltpu.make_async_copy(halo, out_halo, sem.at[1])
+    halo_write.start()
+    halo_write.wait()
     write.wait()
 
 
 def finish_kernel(
     inner,
-    halo, near_hbm, own_hbm, bases_hbm, transfers_hbm, field,
+    halo, near_hbm, own_hbm, bases_hbm, transfers_hbm, field_hbm,
     out, arrived,
-    near, own, bases, transfers, leaf_fields, load_sem, store_sem, send_sem, recv_sem,
+    near, own, bases, transfers, field, leaf_fields, load_sem, store_sem, send_sem, recv_sem,
 ):
     me = lax.axis_index("inner")
     right, left = lax.rem(me + 1, inner), lax.rem(me + inner - 1, inner)
@@ -341,7 +349,10 @@
     barrier = pltpu.get_barrier_semaphore()
     for peer in (left, right):
         pl.semaphore_signal(barrier, inc=1, device_id={"inner": peer}, device_id_type=MESH)
-    loads = [pltpu.make_async_copy(transfers_hbm, transfers, load_sem.at[0])]
+    loads = [
+        pltpu.make_async_copy(transfers_hbm, transfers, load_sem.at[0]),
+        pltpu.make_async_copy(field_hbm, field, load_sem.at[1 + 3 * (leaves // chunk)]),
+    ]
     near_loads, own_loads, base_loads = [], [], []
     for k in range(parts):
         span = pl.ds(k * width, width)
@@ -355,7 +366,8 @@
         own_loads.append(
             pltpu.make_async_copy(own_hbm.at[:, span], own.at[:, span], load_sem.at[1 + 2 * parts + k])
         )
-    loads[0].start()
+    for copy in loads:
+        copy.start()
     for group in zip(base_loads, near_loads, own_loads):
         for copy in group:
             copy.start()
@@ -368,7 +380,8 @@
         )
         copy.start()
         copies.append(copy)
-    loads[0].wait()
+    for copy in loads:
+        copy.wait()
     leaf_fields[...] = dot(field[...], transfers[...], 1, 1).astype(BF)
     stores = []
     for k in range(parts):
@@ -385,6 +398,19 @@
         stores.append(store)
     for copy in stores + copies:
         copy.wait()
+
+
+def rim_kernel(steps, main, arrived, out):
+    rim = arrived.shape[2]
+    out[...] = main[...]
+
+    @pl.when(pl.program_id(0) == 0)
+    def _():
+        out[:, :rim] += arrived[0].astype(F32)
+
+    @pl.when(pl.program_id(0) == steps - 1)
+    def _():
+        out[:, out.shape[1] - rim :] += arrived[1].astype(F32)
 
 
 def on_device(
@@ -412,29 +438,31 @@
             jax.ShapeDtypeStruct((rhs, count), F32),
             jax.ShapeDtypeStruct((rhs, rank), BF),
         ],
-        in_specs=[ANY] * 4 + [VMEM] * 3 + [SMEM],
-        out_specs=[ANY, ANY, VMEM, VMEM],
+        in_specs=[ANY] * 7 + [SMEM],
+        out_specs=[ANY, ANY, ANY, VMEM],
         scratch_shapes=[
             pltpu.VMEM((dim, count), BF),
             pltpu.VMEM((rhs, count), BF),
             pltpu.VMEM((leaves, leaf, rank), BF),
             pltpu.VMEM((leaves * rank, rank), BF),
+            pltpu.VMEM((rank, rank), BF),
+            pltpu.VMEM(couplings.shape[1:], BF),
+            pltpu.VMEM(group_couplings.shape[1:], BF),
+            pltpu.VMEM((rhs, count), F32),
             pltpu.VMEM((rhs, leaves * rank), BF),
             pltpu.VMEM((rhs, rank), F32),
             pltpu.VMEM((inner, rhs, rank), BF),
-            pltpu.VMEM((inner, rhs // ROOTS, rank), F32),
-            pltpu.VMEM((outer, rhs // ROOTS, rank), F32),
+            pltpu.VMEM((outer * inner, rhs // ROOTS, rank), F32),
             pltpu.VMEM((ROOTS, rhs // ROOTS, rank), F32),
             pltpu.VMEM((2, leaf, leaf), BF),
-            dma((3 + parts,)),
+            dma((6 + parts,)),
+            dma((2,)),
             dma((4,)),
             dma((4,)),
             dma((inner,)),
             dma((inner,)),
-            dma((ROOTS,)),
-            dma((inner,)),
-            dma((outer,)),
-            dma((outer,)),
+            dma((ROOTS * outer,)),
+            dma((outer * inner,)),
             dma((inner,)),
             dma((ROOTS,)),
         ],
@@ -450,7 +478,7 @@
             jax.ShapeDtypeStruct((2, rhs, rim), BF),
         ],
         in_specs=[SMEM, SMEM] + [ANY] * 4,
-        out_specs=[ANY, VMEM],
+        out_specs=[ANY, ANY],
         scratch_shapes=[
             pltpu.VMEM((dim, wide), BF),
             pltpu.VMEM((rhs, wide), BF),
@@ -459,6 +487,7 @@
             pltpu.VMEM((rhs, wide), F32),
             pltpu.VMEM((2, leaf, leaf), BF),
             pltpu.VMEM((2, leaf, leaf), BF),
+            pltpu.VMEM((2, rhs, rim), BF),
             dma((5 + parts,)),
         ],
         compiler_params=pltpu.CompilerParams(vmem_limit_bytes=LIMIT),
@@ -470,15 +499,16 @@
             jax.ShapeDtypeStruct((rhs, count), F32),
             jax.ShapeDtypeStruct((2, rhs, rim), BF),
         ],
-        in_specs=[ANY] * 5 + [VMEM],
+        in_specs=[ANY] * 6,
         out_specs=[ANY, ANY],
         scratch_shapes=[
             pltpu.VMEM((rhs, count), F32),
             pltpu.VMEM((rhs, count), F32),
             pltpu.VMEM((leaves, leaf, rank), BF),
             pltpu.VMEM((leaves * rank, rank), BF),
+            pltpu.VMEM((rhs, rank), BF),
             pltpu.VMEM((rhs, leaves * rank), BF),
-            dma((1 + 3 * parts,)),
+            dma((2 + 3 * parts,)),
             dma((parts,)),
             dma((2,)),
             dma((2,)),
@@ -488,8 +518,20 @@
         ),
         name="finish",
     )(halo, near, own, leaf_bases, flat_transfers, field)
-    middle = jnp.zeros((rhs, count - 2 * rim), F32)
-    out = main + jnp.concatenate([arrived[0].astype(F32), middle, arrived[1].astype(F32)], 1)
+    steps = 4
+    width = count // steps
+    out = pl.pallas_call(
+        functools.partial(rim_kernel, steps),
+        out_shape=jax.ShapeDtypeStruct((rhs, count), F32),
+        grid=(steps,),
+        in_specs=[
+            pl.BlockSpec((rhs, width), lambda i: (0, i)),
+            pl.BlockSpec((2, rhs, rim), lambda i: (0, 0, 0)),
+        ],
+        out_specs=pl.BlockSpec((rhs, width), lambda i: (0, i)),
+        compiler_params=pltpu.CompilerParams(vmem_limit_bytes=LIMIT),
+        name="rims",
+    )(main, arrived)
     return jnp.swapaxes(out, 0, 1)[None]
 
 

time: 70.1 us -> 66.5 us (0.949)
  the two profiles are of different devices: /device:TPU:16 before, /device:TPU:24 now
where the time goes in v5:
time: 66.5 us; the launch traced here: 66.3 us
  Pallas kernels  65.6 us (99%)
  between operations  0.68 us (1%)
    pallas_call x1, Pallas kernels, on_device(): pl.pallas_call(functools.partial(pair_kernel, leaves, leaf), out_shape=[j...  24 us
    pallas_call x1, Pallas kernels, on_device(): pl.pallas_call(functools.partial(exchange_kernel, inner, outer, leaves),...  22.2 us
    pallas_call x1, Pallas kernels, on_device(): pl.pallas_call(functools.partial(finish_kernel, inner), out_shape=[jax.Sh...  16.1 us
    pallas_call x1, Pallas kernels, on_device(): pl.pallas_call(functools.partial(rim_kernel, steps), out_shape=jax.ShapeD...  3.43 us

profile of v5, /device:TPU:24, one launch (start us, length us, event | category | flops | bytes accessed | tf_op | source)
XLA Modules:
  0.0 66.3 jit_solution(2823852811697097771)
XLA Ops:
  0.7 22.2 %exchange.1 = (bf16[2,64,2048]{2,1,0:T(8,128)(2,1)}, bf16[2,16,2048]{2,1,0:T(8,128)(2,1)}, f32[16,16384]{1,0:T(8,128)}, bf16[16,128]{1,0:T(8,128)(2,1)}) custom-call(bf16[64,16384]{1,0:T(8,128)(2,1)} %bitcast.19, bf16[16,16384]{1,0:T(8,128)(2,1)} %bitcast.23, bf16[32,512,128]{2,1,0:T(8,128)(2,1)} %bitcast.17, bf16[4096,128]{1,0:T(8,128)(2,1)} %bitcast.21, ...), custom_call_target="tpu_custom_call" | custom-call | tf_op jit(solution)/shard_map/exchange/pallas_call | solution.py:433
  22.8 24.0 %pairs.1 = (f32[16,16384]{1,0:T(8,128)}, bf16[2,16,2048]{2,1,0:T(8,128)(2,1)}) custom-call(s32[2,96]{1,0:T(2,128)} %bitcast.28, s32[1,1]{1,0:T(1,128)S(6)} %copy.11.live, bf16[64,16384]{1,0:T(8,128)(2,1)} %bitcast.20, bf16[16,16384]{1,0:T(8,128)(2,1)} %bitcast.24, bf16[2,64,2048]{2,1,0:T(8,128)(2,1)} %get-tuple-element.13.halo_points, ...), custom_call_target="tpu_custom_call" | custom-call | tf_op jit(solution)/shard_map/pairs/pallas_call | solution.py:474
  46.8 16.1 %finish.1 = (f32[16,16384]{1,0:T(8,128)}, bf16[2,16,2048]{2,1,0:T(8,128)(2,1)}) custom-call(bf16[2,16,2048]{2,1,0:T(8,128)(2,1)} %get-tuple-element.15.halo, f32[16,16384]{1,0:T(8,128)} %get-tuple-element.16.near_hbm, f32[16,16384]{1,0:T(8,128)} %get-tuple-element.17.own_hbm, bf16[32,512,128]{2,1,0:T(8,128)(2,1)} %bitcast.18, bf16[4096,128]{1,0:T(8,128)(2,1)} %bitcast.22, ...), custom_call_target="tpu_custom_call" | custom-call | tf_op jit(solution)/shard_map/finish/pallas_call | solution.py:496
  62.9 3.4 %rims.1 = f32[16,16384]{1,0:T(8,128)} custom-call(f32[16,16384]{1,0:T(8,128)} %get-tuple-element.19.main, bf16[2,16,2048]{2,1,0:T(8,128)(2,1)} %get-tuple-element.20.arrived), custom_call_target="tpu_custom_call" | custom-call | tf_op jit(solution)/shard_map/rims/pallas_call | solution.py:523

commit v6 on v5

--- a/solution.py
+++ b/solution.py
@@ -11,7 +11,7 @@
 RIDGE = 0.25
 EXTRA = 16
 GROUP = 4
-ROOTS = 2
+PAIR_GROUPS = (8, 4, 1)
 BF = jnp.bfloat16
 F32 = jnp.float32
 VMEM = pl.BlockSpec(memory_space=pltpu.VMEM)
@@ -58,7 +58,7 @@
     pt_hbm, ct_hbm, bases_hbm, transfers_hbm, parent_hbm, couplings_hbm, group_couplings_hbm, far,
     halo_points, halo_charges, near_hbm, field_out,
     points, charges, bases, transfers, parent, couplings, group_couplings, near,
-    skeletons, term, slots, gathered, group_field, tiles,
+    skeletons, term, slots, gathered, parts, tiles,
     load_sem, near_sem, halo_send, halo_recv, node_send, node_recv, term_send, term_recv,
     field_send, field_recv,
 ):
@@ -69,11 +69,10 @@
     rim = REACH * leaf
     rank = parent.shape[1]
     chunk = 8
-    rows = rhs // ROOTS
-    roots = [h * (inner // ROOTS) for h in range(ROOTS)]
-    is_root = functools.reduce(jnp.logical_or, [me == root for root in roots])
+    roots = [k * (inner // outer + 2) % inner for k in range(outer - 1)]
     peers = [lax.rem(me + k, inner) for k in range(1, inner)]
-    others = [lax.rem(group + k, outer) for k in range(1, outer)]
+    sources = [lax.rem(group + k, outer) for k in range(1, outer)]
+    sinks = [lax.rem(group + outer - k, outer) for k in range(1, outer)]
     loads = [
         pltpu.make_async_copy(ct_hbm, charges, load_sem.at[0]),
         pltpu.make_async_copy(transfers_hbm, transfers, load_sem.at[1]),
@@ -94,19 +93,20 @@
     for k in (1, 3, 2, 4, 5):
         loads[k].start()
     barrier = pltpu.get_barrier_semaphore()
+    for root, source in zip(roots, sources):
+
+        @pl.when(me == root)
+        def _(source=source):
+            def greet(index, carry):
+                pl.semaphore_signal(
+                    barrier, inc=1, device_id={"inner": index, "outer": source}, device_id_type=MESH
+                )
+                return carry
+
+            lax.fori_loop(0, inner, greet, 0)
+
     for peer in peers:
         pl.semaphore_signal(barrier, inc=1, device_id={"inner": peer}, device_id_type=MESH)
-
-    @pl.when(is_root)
-    def _():
-        def greet(index, carry):
-            for other in others:
-                pl.semaphore_signal(
-                    barrier, inc=1, device_id={"inner": index, "outer": other}, device_id_type=MESH
-                )
-            return carry
-
-        lax.fori_loop(0, inner, greet, 0)
 
     loads[0].wait()
     for k, copy in enumerate(base_loads):
@@ -119,7 +119,7 @@
     slots[me] = node
     loads[3].wait()
     term[...] = dot(node, parent[...], 1, 0)
-    pl.semaphore_wait(barrier, inner - 1 + ROOTS * (outer - 1))
+    pl.semaphore_wait(barrier, inner - 1 + outer - 1)
 
     def remote(source, target, send, recv, **where):
         return pltpu.make_async_remote_copy(
@@ -127,14 +127,9 @@
             device_id=where, device_id_type=MESH,
         )
 
-    mine = group * inner + me
     term_copies = [
-        remote(
-            term.at[pl.ds(h * rows, rows)], gathered.at[mine],
-            term_send.at[h * outer + k], term_recv.at[mine], inner=root, outer=other,
-        )
-        for h, root in enumerate(roots)
-        for k, other in enumerate(others)
+        remote(term, gathered.at[me], term_send.at[k], term_recv.at[me], inner=root, outer=sink)
+        for k, (root, sink) in enumerate(zip(roots, sinks))
     ]
     for copy in term_copies:
         copy.start()
@@ -155,10 +150,10 @@
     ]
     field_copies = [
         [
-            remote(group_field.at[h], group_field.at[h], field_send.at[k], field_recv.at[h], inner=peer)
+            remote(parts.at[h], parts.at[h], field_send.at[k], field_recv.at[h], inner=peer)
             for k, peer in enumerate(peers)
         ]
-        for h in range(ROOTS)
+        for h in range(outer - 1)
     ]
     for copy in halo_copies + node_copies:
         copy.start()
@@ -202,18 +197,13 @@
 
         @pl.when(me == root)
         def _(h=h):
-            part = jnp.zeros((rows, rank), F32)
-            for other in others:
-
-                def arrive(index, carry):
-                    sender = other * inner + index
-                    pltpu.make_async_copy(gathered.at[mine], gathered.at[sender], term_recv.at[sender]).wait()
-                    return carry
-
-                lax.fori_loop(0, inner, arrive, 0)
-                skeleton = jnp.sum(gathered[pl.ds(other * inner, inner)], 0).astype(BF)
-                part += dot(skeleton, group_couplings[other], 1, 1)
-            group_field[h] = part.astype(BF).astype(F32)
+            def arrive(index, carry):
+                pltpu.make_async_copy(term, gathered.at[index], term_recv.at[index]).wait()
+                return carry
+
+            lax.fori_loop(0, inner, arrive, 0)
+            skeleton = jnp.sum(gathered[...], 0).astype(BF)
+            parts[h] = dot(skeleton, group_couplings[sources[h]], 1, 1)
             for copy in field_copies[h]:
                 copy.start()
 
@@ -228,10 +218,10 @@
 
         @pl.when(me != root)
         def _(h=h):
-            pltpu.make_async_copy(group_field.at[h], group_field.at[h], field_recv.at[h]).wait()
-
-    whole = jnp.concatenate([group_field[h] for h in range(ROOTS)], 0).astype(BF)
-    field_out[...] = (field + dot(whole, parent[...], 1, 1)).astype(BF)
+            pltpu.make_async_copy(parts.at[h], parts.at[h], field_recv.at[h]).wait()
+
+    group_field = jnp.sum(parts[...], 0).astype(BF)
+    field_out[...] = (field + dot(group_field, parent[...], 1, 1)).astype(BF)
     for copy in term_copies + node_copies:
         copy.wait_send()
     for h, root in enumerate(roots):
@@ -308,22 +298,21 @@
         totals[:, cols_b] += dot(charges[:, cols_a], tiles[slot], 1, 0)
         totals[:, cols_a] += dot(charges[:, cols_b], flipped[slot], 1, 0)
 
-    def block(index, carry):
-        for k in range(GROUP):
-            at = index * GROUP + k
-            make(at + 1, (k + 1) % 2)
-            use(at, k % 2)
-        return carry
-
-    def single(index, carry):
-        make(index + 1, lax.rem(index + 1, 2))
-        use(index, lax.rem(index, 2))
-        return carry
-
     make(0, 0)
-    whole = number // GROUP
-    lax.fori_loop(0, whole, block, 0)
-    lax.fori_loop(whole * GROUP, number, single, 0)
+    done = 0
+    for size in PAIR_GROUPS:
+
+        def block(index, carry, size=size, done=done):
+            for k in range(size):
+                at = done + index * size + k
+                slot = k % 2 if size > 1 else lax.rem(at, 2)
+                make(at + 1, 1 - slot)
+                use(at, slot)
+            return carry
+
+        blocks = (number - done) // size
+        lax.fori_loop(0, blocks, block, 0)
+        done += blocks * size
     write = pltpu.make_async_copy(totals.at[:, own], out_near, sem.at[0])
     write.start()
     for k, spot in enumerate(spots):
@@ -400,17 +389,33 @@
         copy.wait()
 
 
-def rim_kernel(steps, main, arrived, out):
+def rim_kernel(steps, main_hbm, arrived_hbm, out_hbm, main, arrived, load_sem, rim_sem, store_sem):
+    count = main.shape[1]
     rim = arrived.shape[2]
-    out[...] = main[...]
-
-    @pl.when(pl.program_id(0) == 0)
-    def _():
-        out[:, :rim] += arrived[0].astype(F32)
-
-    @pl.when(pl.program_id(0) == steps - 1)
-    def _():
-        out[:, out.shape[1] - rim :] += arrived[1].astype(F32)
+    width = count // steps
+    spans = [pl.ds(k * width, width) for k in range(steps)]
+    loads = [
+        pltpu.make_async_copy(main_hbm.at[:, span], main.at[:, span], load_sem.at[k])
+        for k, span in enumerate(spans)
+    ]
+    stores = [
+        pltpu.make_async_copy(main.at[:, span], out_hbm.at[:, span], store_sem.at[k])
+        for k, span in enumerate(spans)
+    ]
+    rims = pltpu.make_async_copy(arrived_hbm, arrived, rim_sem)
+    rims.start()
+    for copy in loads:
+        copy.start()
+    rims.wait()
+    for k in range(steps):
+        loads[k].wait()
+        if k == 0:
+            main[:, :rim] += arrived[0].astype(F32)
+        if k == steps - 1:
+            main[:, count - rim :] += arrived[1].astype(F32)
+        stores[k].start()
+    for copy in stores:
+        copy.wait()
 
 
 def on_device(
@@ -452,8 +457,8 @@
             pltpu.VMEM((rhs, leaves * rank), BF),
             pltpu.VMEM((rhs, rank), F32),
             pltpu.VMEM((inner, rhs, rank), BF),
-            pltpu.VMEM((outer * inner, rhs // ROOTS, rank), F32),
-            pltpu.VMEM((ROOTS, rhs // ROOTS, rank), F32),
+            pltpu.VMEM((inner, rhs, rank), F32),
+            pltpu.VMEM((outer - 1, rhs, rank), F32),
             pltpu.VMEM((2, leaf, leaf), BF),
             dma((6 + parts,)),
             dma((2,)),
@@ -461,10 +466,10 @@
             dma((4,)),
             dma((inner,)),
             dma((inner,)),
-            dma((ROOTS * outer,)),
-            dma((outer * inner,)),
+            dma((outer - 1,)),
             dma((inner,)),
-            dma((ROOTS,)),
+            dma((inner,)),
+            dma((outer - 1,)),
         ],
         compiler_params=pltpu.CompilerParams(
             vmem_limit_bytes=LIMIT, collective_id=0, has_side_effects=True
@@ -519,16 +524,18 @@
         name="finish",
     )(halo, near, own, leaf_bases, flat_transfers, field)
     steps = 4
-    width = count // steps
     out = pl.pallas_call(
         functools.partial(rim_kernel, steps),
         out_shape=jax.ShapeDtypeStruct((rhs, count), F32),
-        grid=(steps,),
-        in_specs=[
-            pl.BlockSpec((rhs, width), lambda i: (0, i)),
-            pl.BlockSpec((2, rhs, rim), lambda i: (0, 0, 0)),
-        ],
-        out_specs=pl.BlockSpec((rhs, width), lambda i: (0, i)),
+        in_specs=[ANY, ANY],
+        out_specs=ANY,
+        scratch_shapes=[
+            pltpu.VMEM((rhs, count), F32),
+            pltpu.VMEM((2, rhs, rim), BF),
+            dma((steps,)),
+            dma,
+            dma((steps,)),
+        ],
         compiler_params=pltpu.CompilerParams(vmem_limit_bytes=LIMIT),
         name="rims",
     )(main, arrived)

time: 66.5 us -> 64 us (0.962)
  the two profiles are of different devices: /device:TPU:24 before, /device:TPU:16 now
where the time goes in v6:
time: 64 us; the launch traced here: 63.9 us
  Pallas kernels  63.2 us (99%)
  between operations  0.68 us (1%)
    pallas_call x1, Pallas kernels, on_device(): pl.pallas_call(functools.partial(pair_kernel, leaves, leaf), out_shape=[j...  32.8 us
    pallas_call x1, Pallas kernels, on_device(): pl.pallas_call(functools.partial(exchange_kernel, inner, outer, leaves),...  20.6 us
    pallas_call x1, Pallas kernels, on_device(): pl.pallas_call(functools.partial(finish_kernel, inner), out_shape=[jax.Sh...  7.61 us
    pallas_call x1, Pallas kernels, on_device(): pl.pallas_call(functools.partial(rim_kernel, steps), out_shape=jax.ShapeD...  2.19 us

profile of v6, /device:TPU:16, one launch (start us, length us, event | category | flops | bytes accessed | tf_op | source)
XLA Modules:
  0.0 63.9 jit_solution(2586807493642856173)
XLA Ops:
  0.7 20.6 %exchange.1 = (bf16[2,64,2048]{2,1,0:T(8,128)(2,1)}, bf16[2,16,2048]{2,1,0:T(8,128)(2,1)}, f32[16,16384]{1,0:T(8,128)}, bf16[16,128]{1,0:T(8,128)(2,1)}) custom-call(bf16[64,16384]{1,0:T(8,128)(2,1)} %bitcast.19, bf16[16,16384]{1,0:T(8,128)(2,1)} %bitcast.23, bf16[32,512,128]{2,1,0:T(8,128)(2,1)} %bitcast.17, bf16[4096,128]{1,0:T(8,128)(2,1)} %bitcast.21, ...), custom_call_target="tpu_custom_call" | custom-call | tf_op jit(solution)/shard_map/exchange/pallas_call | solution.py:438
  21.3 32.8 %pairs.1 = (f32[16,16384]{1,0:T(8,128)}, bf16[2,16,2048]{2,1,0:T(8,128)(2,1)}) custom-call(s32[2,96]{1,0:T(2,128)} %bitcast.28, s32[1,1]{1,0:T(1,128)S(6)} %copy.11.live, bf16[64,16384]{1,0:T(8,128)(2,1)} %bitcast.20, bf16[16,16384]{1,0:T(8,128)(2,1)} %bitcast.24, bf16[2,64,2048]{2,1,0:T(8,128)(2,1)} %get-tuple-element.13.halo_points, ...), custom_call_target="tpu_custom_call" | custom-call | tf_op jit(solution)/shard_map/pairs/pallas_call | solution.py:479
  54.1 7.6 %finish.1 = (f32[16,16384]{1,0:T(8,128)}, bf16[2,16,2048]{2,1,0:T(8,128)(2,1)}) custom-call(bf16[2,16,2048]{2,1,0:T(8,128)(2,1)} %get-tuple-element.15.halo, f32[16,16384]{1,0:T(8,128)} %get-tuple-element.16.near_hbm, f32[16,16384]{1,0:T(8,128)} %get-tuple-element.17.own_hbm, bf16[32,512,128]{2,1,0:T(8,128)(2,1)} %bitcast.18, bf16[4096,128]{1,0:T(8,128)(2,1)} %bitcast.22, ...), custom_call_target="tpu_custom_call" | custom-call | tf_op jit(solution)/shard_map/finish/pallas_call | solution.py:501
  61.7 2.2 %rims.1 = f32[16,16384]{1,0:T(8,128)} custom-call(f32[16,16384]{1,0:T(8,128)} %get-tuple-element.19.main_hbm, bf16[2,16,2048]{2,1,0:T(8,128)(2,1)} %get-tuple-element.20.arrived_hbm), custom_call_target="tpu_custom_call" | custom-call | tf_op jit(solution)/shard_map/rims/pallas_call | solution.py:527

commit v7 on v6

--- a/solution.py
+++ b/solution.py
@@ -17,8 +17,8 @@
 VMEM = pl.BlockSpec(memory_space=pltpu.VMEM)
 SMEM = pl.BlockSpec(memory_space=pltpu.SMEM)
 ANY = pl.BlockSpec(memory_space=pl.ANY)
+HBM = pl.BlockSpec(memory_space=pltpu.HBM)
 MESH = pl.DeviceIdType.MESH
-LIMIT = 56 * 2**20
 
 
 def dot(left, right, left_dim, right_dim):
@@ -69,7 +69,10 @@
     rim = REACH * leaf
     rank = parent.shape[1]
     chunk = 8
-    roots = [k * (inner // outer + 2) % inner for k in range(outer - 1)]
+    half = inner // 2
+    roots = [
+        (k, h, h * half + k * (half // (outer - 1))) for k in range(outer - 1) for h in range(2)
+    ]
     peers = [lax.rem(me + k, inner) for k in range(1, inner)]
     sources = [lax.rem(group + k, outer) for k in range(1, outer)]
     sinks = [lax.rem(group + outer - k, outer) for k in range(1, outer)]
@@ -90,13 +93,13 @@
     loads[0].start()
     for copy in base_loads:
         copy.start()
-    for k in (1, 3, 2, 4, 5):
-        loads[k].start()
+    loads[1].start()
+    loads[3].start()
     barrier = pltpu.get_barrier_semaphore()
-    for root, source in zip(roots, sources):
+    for k, _, root in roots:
 
         @pl.when(me == root)
-        def _(source=source):
+        def _(source=sources[k]):
             def greet(index, carry):
                 pl.semaphore_signal(
                     barrier, inc=1, device_id={"inner": index, "outer": source}, device_id_type=MESH
@@ -114,12 +117,14 @@
         for index in range(k * chunk, (k + 1) * chunk):
             block = charges[:, index * leaf : (index + 1) * leaf]
             skeletons[:, index * rank : (index + 1) * rank] = dot(block, bases[index], 1, 0).astype(BF)
+    for k in (2, 4, 5):
+        loads[k].start()
     loads[1].wait()
     node = dot(skeletons[...], transfers[...], 1, 0).astype(BF)
     slots[me] = node
     loads[3].wait()
     term[...] = dot(node, parent[...], 1, 0)
-    pl.semaphore_wait(barrier, inner - 1 + outer - 1)
+    pl.semaphore_wait(barrier, inner - 1 + len(roots))
 
     def remote(source, target, send, recv, **where):
         return pltpu.make_async_remote_copy(
@@ -128,8 +133,8 @@
         )
 
     term_copies = [
-        remote(term, gathered.at[me], term_send.at[k], term_recv.at[me], inner=root, outer=sink)
-        for k, (root, sink) in enumerate(zip(roots, sinks))
+        remote(term, gathered.at[me], term_send.at[at], term_recv.at[me], inner=root, outer=sinks[k])
+        for at, (k, _, root) in enumerate(roots)
     ]
     for copy in term_copies:
         copy.start()
@@ -150,10 +155,11 @@
     ]
     field_copies = [
         [
-            remote(parts.at[h], parts.at[h], field_send.at[k], field_recv.at[h], inner=peer)
-            for k, peer in enumerate(peers)
+            remote(parts.at[k], parts.at[k], field_send.at[peer], field_recv.at[k], inner=peer)
+            for peer in range(h * half, (h + 1) * half)
+            if peer != root
         ]
-        for h in range(outer - 1)
+        for k, h, root in roots
     ]
     for copy in halo_copies + node_copies:
         copy.start()
@@ -183,7 +189,7 @@
 
     own_tile(0, 0)
     total = leaves // GROUP
-    stop = 5 * total // 8
+    stop = 3 * total // 8
     lax.fori_loop(0, stop, diagonal, 0)
     spans = [pl.ds(0, stop * GROUP * leaf), pl.ds(stop * GROUP * leaf, (total - stop) * GROUP * leaf)]
     near_copies = [
@@ -193,18 +199,18 @@
     near_copies[0].start()
     loads[4].wait()
     loads[5].wait()
-    for h, root in enumerate(roots):
+    for at, (k, _, root) in enumerate(roots):
 
         @pl.when(me == root)
-        def _(h=h):
+        def _(at=at, k=k):
             def arrive(index, carry):
                 pltpu.make_async_copy(term, gathered.at[index], term_recv.at[index]).wait()
                 return carry
 
             lax.fori_loop(0, inner, arrive, 0)
             skeleton = jnp.sum(gathered[...], 0).astype(BF)
-            parts[h] = dot(skeleton, group_couplings[sources[h]], 1, 1)
-            for copy in field_copies[h]:
+            parts[k] = dot(skeleton, group_couplings[sources[k]], 1, 1)
+            for copy in field_copies[at]:
                 copy.start()
 
     lax.fori_loop(stop, total, diagonal, 0)
@@ -214,21 +220,22 @@
     field = jnp.zeros((rhs, rank), F32)
     for j in range(couplings.shape[0]):
         field += dot(slots[far[0, j]], couplings[j], 1, 1)
-    for h, root in enumerate(roots):
-
-        @pl.when(me != root)
-        def _(h=h):
-            pltpu.make_async_copy(parts.at[h], parts.at[h], field_recv.at[h]).wait()
+    for k in range(outer - 1):
+        first_root, second_root = [root for at, _, root in roots if at == k]
+
+        @pl.when((me != first_root) & (me != second_root))
+        def _(k=k):
+            pltpu.make_async_copy(parts.at[k], parts.at[k], field_recv.at[k]).wait()
 
     group_field = jnp.sum(parts[...], 0).astype(BF)
     field_out[...] = (field + dot(group_field, parent[...], 1, 1)).astype(BF)
     for copy in term_copies + node_copies:
         copy.wait_send()
-    for h, root in enumerate(roots):
+    for at, (_, _, root) in enumerate(roots):
 
         @pl.when(me == root)
-        def _(h=h):
-            for copy in field_copies[h]:
+        def _(at=at):
+            for copy in field_copies[at]:
                 copy.wait_send()
 
     for copy in near_copies:
@@ -443,7 +450,7 @@
             jax.ShapeDtypeStruct((rhs, count), F32),
             jax.ShapeDtypeStruct((rhs, rank), BF),
         ],
-        in_specs=[ANY] * 7 + [SMEM],
+        in_specs=[HBM] * 7 + [SMEM],
         out_specs=[ANY, ANY, ANY, VMEM],
         scratch_shapes=[
             pltpu.VMEM((dim, count), BF),
@@ -466,13 +473,13 @@
             dma((4,)),
             dma((inner,)),
             dma((inner,)),
-            dma((outer - 1,)),
+            dma((2 * (outer - 1),)),
             dma((inner,)),
             dma((inner,)),
             dma((outer - 1,)),
         ],
         compiler_params=pltpu.CompilerParams(
-            vmem_limit_bytes=LIMIT, collective_id=0, has_side_effects=True
+            vmem_limit_bytes=56 * 2**20, collective_id=0, has_side_effects=True
         ),
         name="exchange",
     )(pt, ct, leaf_bases, flat_transfers, parents[0, 0], couplings[0], group_couplings[0], far_list)
@@ -495,7 +502,7 @@
             pltpu.VMEM((2, rhs, rim), BF),
             dma((5 + parts,)),
         ],
-        compiler_params=pltpu.CompilerParams(vmem_limit_bytes=LIMIT),
+        compiler_params=pltpu.CompilerParams(vmem_limit_bytes=56 * 2**20),
         name="pairs",
     )(pairs, pair_count, pt, ct, halo_points, halo_charges)
     main, arrived = pl.pallas_call(
@@ -504,7 +511,7 @@
             jax.ShapeDtypeStruct((rhs, count), F32),
             jax.ShapeDtypeStruct((2, rhs, rim), BF),
         ],
-        in_specs=[ANY] * 6,
+        in_specs=[ANY] * 3 + [HBM, HBM, ANY],
         out_specs=[ANY, ANY],
         scratch_shapes=[
             pltpu.VMEM((rhs, count), F32),
@@ -519,7 +526,7 @@
             dma((2,)),
         ],
         compiler_params=pltpu.CompilerParams(
-            vmem_limit_bytes=LIMIT, collective_id=1, has_side_effects=True
+            vmem_limit_bytes=56 * 2**20, collective_id=1, has_side_effects=True
         ),
         name="finish",
     )(halo, near, own, leaf_bases, flat_transfers, field)
@@ -528,7 +535,7 @@
         functools.partial(rim_kernel, steps),
         out_shape=jax.ShapeDtypeStruct((rhs, count), F32),
         in_specs=[ANY, ANY],
-        out_specs=ANY,
+        out_specs=HBM,
         scratch_shapes=[
             pltpu.VMEM((rhs, count), F32),
             pltpu.VMEM((2, rhs, rim), BF),
@@ -536,7 +543,7 @@
             dma,
             dma((steps,)),
         ],
-        compiler_params=pltpu.CompilerParams(vmem_limit_bytes=LIMIT),
+        compiler_params=pltpu.CompilerParams(vmem_limit_bytes=56 * 2**20),
         name="rims",
     )(main, arrived)
     return jnp.swapaxes(out, 0, 1)[None]

time: 64 us -> 61 us (0.953)
  Pallas kernels: 63.2 us -> 60.2 us
    pallas_call x1, Pallas kernels: 32.8 us -> 12 us  [on_device(): pl.pallas_call(functools.partial(pair_kernel, leaves, leaf), out_shape=[j...]
    pallas_call x1, Pallas kernels: 7.61 us -> 25.3 us  [on_device(): pl.pallas_call(functools.partial(finish_kernel, inner), out_shape=[jax.Sh...]
where the time goes in v7:
time: 61 us; the launch traced here: 60.8 us
  Pallas kernels  60.2 us (99%)
  between operations  0.68 us (1%)
    pallas_call x1, Pallas kernels, on_device(): pl.pallas_call(functools.partial(finish_kernel, inner), out_shape=[jax.Sh...  25.3 us
    pallas_call x1, Pallas kernels, on_device(): pl.pallas_call(functools.partial(exchange_kernel, inner, outer, leaves),...  20.6 us
    pallas_call x1, Pallas kernels, on_device(): pl.pallas_call(functools.partial(pair_kernel, leaves, leaf), out_shape=[j...  12 us
    pallas_call x1, Pallas kernels, on_device(): pl.pallas_call(functools.partial(rim_kernel, steps), out_shape=jax.ShapeD...  2.19 us

profile of v7, /device:TPU:16, one launch (start us, length us, event | category | flops | bytes accessed | tf_op | source)
XLA Modules:
  0.0 60.8 jit_solution(9083719375408238488)
XLA Ops:
  0.7 20.6 %exchange.1 = (bf16[2,64,2048]{2,1,0:T(8,128)(2,1)}, bf16[2,16,2048]{2,1,0:T(8,128)(2,1)}, f32[16,16384]{1,0:T(8,128)}, bf16[16,128]{1,0:T(8,128)(2,1)}) custom-call(bf16[64,16384]{1,0:T(8,128)(2,1)} %bitcast.19, bf16[16,16384]{1,0:T(8,128)(2,1)} %bitcast.23, bf16[32,512,128]{2,1,0:T(8,128)(2,1)} %bitcast.17, bf16[4096,128]{1,0:T(8,128)(2,1)} %bitcast.21, ...), custom_call_target="tpu_custom_call" | custom-call | tf_op jit(solution)/shard_map/exchange/pallas_call | solution.py:445
  21.2 12.0 %pairs.1 = (f32[16,16384]{1,0:T(8,128)}, bf16[2,16,2048]{2,1,0:T(8,128)(2,1)}) custom-call(s32[2,96]{1,0:T(2,128)} %bitcast.28, s32[1,1]{1,0:T(1,128)S(6)} %copy.11.live, bf16[64,16384]{1,0:T(8,128)(2,1)} %bitcast.20, bf16[16,16384]{1,0:T(8,128)(2,1)} %bitcast.24, bf16[2,64,2048]{2,1,0:T(8,128)(2,1)} %get-tuple-element.13.halo_points, ...), custom_call_target="tpu_custom_call" | custom-call | tf_op jit(solution)/shard_map/pairs/pallas_call | solution.py:486
  33.3 25.3 %finish.1 = (f32[16,16384]{1,0:T(8,128)}, bf16[2,16,2048]{2,1,0:T(8,128)(2,1)}) custom-call(bf16[2,16,2048]{2,1,0:T(8,128)(2,1)} %get-tuple-element.15.halo, f32[16,16384]{1,0:T(8,128)} %get-tuple-element.16.near_hbm, f32[16,16384]{1,0:T(8,128)} %get-tuple-element.17.own_hbm, bf16[32,512,128]{2,1,0:T(8,128)(2,1)} %bitcast.18, bf16[4096,128]{1,0:T(8,128)(2,1)} %bitcast.22, ...), custom_call_target="tpu_custom_call" | custom-call | tf_op jit(solution)/shard_map/finish/pallas_call | solution.py:508
  58.6 2.2 %rims.1 = f32[16,16384]{1,0:T(8,128)} custom-call(f32[16,16384]{1,0:T(8,128)} %get-tuple-element.19.main_hbm, bf16[2,16,2048]{2,1,0:T(8,128)(2,1)} %get-tuple-element.20.arrived_hbm), custom_call_target="tpu_custom_call" | custom-call | tf_op jit(solution)/shard_map/rims/pallas_call | solution.py:534
